TPU v7x, 256 devices: a whole 4x4x8 slice. The times are simulated.
256 devices in a mesh: dp: 8 (over z), seq: 32 (over y, x, core).
Axes of the slice: x: 4, y: 4, z: 8, core: 2. Of those that a mesh axis runs over, the one named last changes fastest.
Arguments:
- queries: bfloat16 [32768, 12288], P(('dp', 'seq')), may hold values from -204 to 204
- kv_latent: bfloat16 [32768, 512], P(('dp', 'seq')), may hold values from -6 to 6
- key_rope: bfloat16 [32768, 64], P(('dp', 'seq')), may hold values from -6 to 6
- kv_gain: float32 [512], replicated, may hold values from 0.1 to 1.9
- kv_up: bfloat16 [512, 16384], P(None, 'seq'), may hold values from -0.25 to 0.25
- segment_blocks: int32 [8], replicated, may hold values from 1 to 8, 32 in all
- bucket_of: int32 [8], replicated, may hold values from 0 to 7, each once
- doc_breaks: int32 [8, 32], replicated, may hold values from 0 to 1, as said below
Outputs:
- attended: bfloat16 [32768, 8192], P(('dp', 'seq'))
Inputs may be any that keep to these rules, and one draw needn't show every extreme that they name: The plan: rollout s's tiles are cut in order into segments of segment_blocks[g] tiles, segment g goes to bucket bucket_of[(s + g) mod 8]. The entries sum to 32, and the largest is exactly 8. `bucket_of`: each bucket number appears once. `doc_breaks`: 1 marks a tile of a rollout where a new document begins; a document also begins at every segment's first tile. Some rollout has no mark and some rollout has every tile marked.
All inputs are finite; a program needn't handle non-finite values.
Results may differ from a plain program's by a relative error of at most 0.012.
The roundings to bfloat16 on the way count: a program that leaves them out, or rounds other values in their place, can miss the bound.
Values may be sent and summed in bfloat16 or wider, within the bound.
A program may use at most 128 MiB of HBM per device.

v0:
```python
import jax
import jax.numpy as jnp
from jax import lax
from jax.sharding import PartitionSpec as P

HD_NOPE = 128
HD_V = 128
BLK = 128


epsilon = 1e-06
row_block = 512


def inverse_of(bucket_of):
    slot_count = bucket_of.shape[0]
    indices = jnp.arange(slot_count, dtype=jnp.int32)
    return jnp.sum(jnp.where(bucket_of[:, None] == indices[None, :], indices[:, None], 0), axis=0)


def segment_starts(segment_blocks):
    return jnp.cumsum(segment_blocks) - segment_blocks


def bucket_layout(segment_blocks, bucket_of, bucket, count_blocks):
    slot_count = segment_blocks.shape[0]
    indices = jnp.arange(slot_count, dtype=jnp.int32)
    starts = segment_starts(segment_blocks)
    segment_of = (inverse_of(bucket_of)[bucket] - indices) % slot_count
    lengths = segment_blocks[segment_of]
    place_end = jnp.cumsum(lengths)
    place_start = place_end - lengths
    block_ids = jnp.arange(count_blocks, dtype=jnp.int32)
    source = jnp.sum((place_end[None, :] <= block_ids[:, None]).astype(jnp.int32), axis=1)
    within = block_ids - place_start[source]
    return (source, within, starts[segment_of[source]] + within)


def first_blocks(starts_here):
    block_ids = jnp.arange(starts_here.shape[0], dtype=jnp.int32)
    return lax.cummax(jnp.where(starts_here, block_ids, 0), axis=0)


def pack_slots(row_data, slot_starts, slot_rows):
    padded = jnp.pad(row_data, ((0, slot_rows), (0, 0)))
    return jax.vmap(lambda begin_row: lax.dynamic_slice_in_dim(padded, begin_row, slot_rows, 0))(
        slot_starts
    )


def unpack_slots(received, source, within):
    slot_count, slot_rows, row_width = received.shape
    per_slot = slot_rows // BLK
    tile_stack = received.reshape(slot_count * per_slot, BLK, row_width)
    picked = jnp.take(tile_stack, source * per_slot + within, axis=0)
    return picked.reshape(-1, row_width)


def attend(query_rows, keyval, rotary, first_row, head_count, lead_rows):
    window = query_rows.shape[0]
    head_dim = query_rows.shape[1] // head_count
    rotary_dim = rotary.shape[1]
    nope_dim = head_dim - rotary_dim
    value_dim = keyval.shape[1] // head_count - nope_dim
    tile_rows = min(row_block, window)
    score_scale = head_dim ** (-0.5)
    query_heads = query_rows.reshape(window, head_count, head_dim)
    key_value = keyval.reshape(window, head_count, nope_dim + value_dim)
    key_heads = jnp.concatenate(
        [
            key_value[:, :, :nope_dim],
            jnp.broadcast_to(rotary[:, None, :], (window, head_count, rotary_dim)),
        ],
        axis=2,
    )
    key_heads = jnp.pad(key_heads, ((lead_rows, 0), (0, 0), (0, 0)))
    value_heads = jnp.pad(key_value[:, :, nope_dim:], ((lead_rows, 0), (0, 0), (0, 0)))

    def scored(first_query, offset, key_rows):
        query_tile = lax.dynamic_slice_in_dim(query_heads, first_query, tile_rows, 0)
        key_tile = lax.dynamic_slice_in_dim(key_heads, first_query + offset, key_rows, 0)
        value_tile = lax.dynamic_slice_in_dim(value_heads, first_query + offset, key_rows, 0)
        query_pos = first_query + jnp.arange(tile_rows, dtype=jnp.int32)
        key_pos = first_query + offset - lead_rows + jnp.arange(key_rows, dtype=jnp.int32)
        doc_firsts = lax.dynamic_slice_in_dim(first_row, first_query, tile_rows, 0)
        allowed = (key_pos[None, :] <= query_pos[:, None]) & (
            key_pos[None, :] >= doc_firsts[:, None]
        )
        scores = (
            jnp.einsum("qhe,khe->hqk", query_tile, key_tile, preferred_element_type=jnp.float32)
            * score_scale
        )
        scores = jnp.where(allowed[None, :, :], scores, jnp.float32(-1e30))
        row_max = jnp.max(scores, axis=2, keepdims=True)
        exponent = jnp.exp(scores - row_max)
        weights = (exponent / jnp.sum(exponent, axis=2, keepdims=True)).astype(jnp.bfloat16)
        attended = jnp.einsum(
            "hqk,khe->qhe", weights, value_tile, preferred_element_type=jnp.float32
        )
        return attended.reshape(tile_rows, head_count * value_dim).astype(jnp.bfloat16)

    def one_block(position):
        first_query = position * tile_rows
        return scored(first_query, 0, tile_rows + lead_rows)

    blocks_out = lax.map(one_block, jnp.arange(window // tile_rows, dtype=jnp.int32))
    return blocks_out.reshape(window, head_count * value_dim)


def on_device(queries, kv_latent, key_rope, kv_gain, kv_up, segment_blocks, bucket_of, doc_breaks):
    buckets = lax.axis_size("dp")
    rollout = lax.axis_index("dp")
    head_count = kv_up.shape[1] // (HD_NOPE + HD_V)
    query_rows = lax.all_to_all(queries, "seq", split_axis=1, concat_axis=0, tiled=True)
    latent, rotary = (
        lax.all_gather(kv_latent, "seq", axis=0, tiled=True),
        lax.all_gather(key_rope, "seq", axis=0, tiled=True),
    )
    window = latent.shape[0]
    count_blocks = window // BLK
    slot_rows = 2 * count_blocks // buckets * BLK
    lead_rows = slot_rows - BLK
    latent_wide = latent.astype(jnp.float32)
    normed = (
        latent_wide
        * lax.rsqrt(jnp.mean(latent_wide * latent_wide, axis=1, keepdims=True) + epsilon)
        * kv_gain
    ).astype(jnp.bfloat16)
    keyval = jnp.dot(normed, kv_up, preferred_element_type=jnp.float32).astype(jnp.bfloat16)
    starts = segment_starts(segment_blocks)
    slot_starts = starts[(inverse_of(bucket_of) - rollout) % buckets] * BLK
    source, within, src_block = bucket_layout(segment_blocks, bucket_of, rollout, count_blocks)
    block_ids = jnp.arange(count_blocks, dtype=jnp.int32)
    starts_here = jnp.any(block_ids[:, None] == starts[None, :], axis=1) | (
        doc_breaks[rollout] == 1
    )
    first_row = jnp.repeat(first_blocks(starts_here) * BLK, BLK)
    local_out = attend(query_rows, keyval, rotary, first_row, head_count, lead_rows)
    received = lax.all_to_all(
        pack_slots(local_out, slot_starts, slot_rows), "dp", split_axis=0, concat_axis=0, tiled=True
    )
    bucketed = unpack_slots(received, source, within)
    return lax.all_to_all(bucketed, "seq", split_axis=0, concat_axis=1, tiled=True)


def solution(mesh):
    in_specs = (
        P(("dp", "seq"), None),
        P(("dp", "seq"), None),
        P(("dp", "seq"), None),
        P(),
        P(None, "seq"),
        P(),
        P(),
        P(),
    )
    out_specs = P(("dp", "seq"), None)
    return jax.shard_map(
        on_device, mesh=mesh, in_specs=in_specs, out_specs=out_specs, check_vma=False
    )
```

profile of v0, /device:TPU:1, one launch (start us, length us, event | category | flops | bytes accessed | tf_op | source)
XLA Modules:
  0.0 364.3 jit_solution(15475114724081940192)
XLA Ops:
  7.3 4.6 %copy.32 = bf16[128,12288]{0,1:T(8,128)(2,1)} copy(bf16[128,12288]{1,0:T(8,128)(2,1)} %param.10) | data formatting | bytes 6291456 | tf_op args[0]
  11.9 8.8 %all-to-all-start = ((bf16[128,32,384]{0,2,1:T(8,128)(2,1)}), bf16[128,32,384]{0,2,1:T(8,128)(2,1)}, u32[]{:S(2)}, u32[]{:S(2)}) async-start(bf16[128,32,384]{0,2,1:T(8,128)(2,1)} %bitcast.64), calls=%async_computation | async-start | bytes 6291456 | tf_op jit(solution)/shard_map/all_to_all | solution.py:114
  22.7 56.2 %all_gather.7 = bf16[4096,64]{0,1:T(8,128)(2,1)S(1)} all-gather(bf16[128,64]{0,1:T(8,128)(2,1)S(1)} %copy-done.3), channel_id=1, replica_groups=mesh['dp'=8,'seq'=32] {'seq'}, dimensions={0}, use_global_device_ids=true | all-gather | bytes 540672 | tf_op jit(solution)/shard_map/all_gather | solution.py:117
  79.1 5.8 %copy.33 = bf16[32,128,384]{1,0,2:T(8,128)(2,1)} copy(bf16[32,128,384]{1,2,0:T(8,128)(2,1)} %bitcast.16) | data formatting | bytes 6291456 | tf_op jit(solution)/shard_map/all_to_all | solution.py:114
  84.8 5.8 %reshape.395 = bf16[4096,2,192]{0,2,1:T(8,128)(2,1)} reshape(bf16[32,128,384]{1,0,2:T(8,128)(2,1)} %copy.33) | data formatting | bytes 6291456 | tf_op jit(solution)/shard_map/reshape | solution.py:67
  90.6 3.2 fusion.42
  94.1 2.9 convolution_convert_fusion
  97.6 2.0 fusion.50
  101.4 87.6 %while.13 = (s32[]{:T(128)}, bf16[8,512,256]{2,1,0:T(8,128)(2,1)}, s32[8]{0:T(128)S(1)}, bf16[4992,2,128]{0,2,1:T(8,128)(2,1)}, s32[4096]{0:T(1024)S(1)}, /*inde...) while((s32[]{:T(128)}, bf16[8,512,256]{2,1,0:T(8,128)(2,1)}, ...), condition=%wide.region_10.11_spmd, body=%wide.region_7.10_spmd.sunk | while | flops 1491670656 | bytes 7175408 | solution.py:106
  103.4 3.7 %fusion.79 = f32[2,512]{1,0:T(2,128)S(1)} fusion(pred[512,1408]{1,0:T(8,128)(4,1)S(1)} %compare_and_fusion.3, bf16[4992,2,192]{0,2,1:T(8,128)(2,1)} %get-tuple-element.227, s32[]{:T(128)S(6)} %select_n.186, bf16[4096,2,192]{0,2,1:T(8,128)(2,1)} %get-tuple-element.226, s32[]{:T(128)S(6)} %select_n.185), kind=kOutput, calls=%fused_computation.85.clone.1 | convolution fusion | flops 559416704 | bytes 2199560 | tf_op jit(solution)/shard_map/while/body/eval_jaxpr/sub | solution.py:95
  107.1 4.4 %fusion.80 = bf16[2,128,512]{2,1,0:T(8,128)(2,1)S(1)} fusion(f32[2,512]{1,0:T(2,128)S(1)} %fusion.79, bf16[4992,2,128]{0,2,1:T(8,128)(2,1)} %get-tuple-element.224, s32[]{:T(128)S(6)} %select_n.186, pred[512,1408]{1,0:T(8,128)(4,1)S(1)} %compare_and_fusion.3, bf16[4992,2,192]{0,2,1:T(8,128)(2,1)} %get-tuple-element.227, ...), kind=kOutput, calls=%fused_computation.14.clone.1 | convolution fusion | flops 930089344 | bytes 3184128 | tf_op jit(solution)/shard_map/while/body/eval_jaxpr/hqk,khe->qhe/dot_general | solution.py:97
  114.4 3.7 %fusion.79 = f32[2,512]{1,0:T(2,128)S(1)} fusion(pred[512,1408]{1,0:T(8,128)(4,1)S(1)} %compare_and_fusion.3, bf16[4992,2,192]{0,2,1:T(8,128)(2,1)} %get-tuple-element.227, s32[]{:T(128)S(6)} %select_n.186, bf16[4096,2,192]{0,2,1:T(8,128)(2,1)} %get-tuple-element.226, s32[]{:T(128)S(6)} %select_n.185), kind=kOutput, calls=%fused_computation.85.clone.1 | convolution fusion | flops 559416704 | bytes 2199560 | tf_op jit(solution)/shard_map/while/body/eval_jaxpr/sub | solution.py:95
  118.1 4.4 %fusion.80 = bf16[2,128,512]{2,1,0:T(8,128)(2,1)S(1)} fusion(f32[2,512]{1,0:T(2,128)S(1)} %fusion.79, bf16[4992,2,128]{0,2,1:T(8,128)(2,1)} %get-tuple-element.224, s32[]{:T(128)S(6)} %select_n.186, pred[512,1408]{1,0:T(8,128)(4,1)S(1)} %compare_and_fusion.3, bf16[4992,2,192]{0,2,1:T(8,128)(2,1)} %get-tuple-element.227, ...), kind=kOutput, calls=%fused_computation.14.clone.1 | convolution fusion | flops 930089344 | bytes 3184128 | tf_op jit(solution)/shard_map/while/body/eval_jaxpr/hqk,khe->qhe/dot_general | solution.py:97
  125.3 3.7 %fusion.79 = f32[2,512]{1,0:T(2,128)S(1)} fusion(pred[512,1408]{1,0:T(8,128)(4,1)S(1)} %compare_and_fusion.3, bf16[4992,2,192]{0,2,1:T(8,128)(2,1)} %get-tuple-element.227, s32[]{:T(128)S(6)} %select_n.186, bf16[4096,2,192]{0,2,1:T(8,128)(2,1)} %get-tuple-element.226, s32[]{:T(128)S(6)} %select_n.185), kind=kOutput, calls=%fused_computation.85.clone.1 | convolution fusion | flops 559416704 | bytes 2199560 | tf_op jit(solution)/shard_map/while/body/eval_jaxpr/sub | solution.py:95
  129.0 4.4 %fusion.80 = bf16[2,128,512]{2,1,0:T(8,128)(2,1)S(1)} fusion(f32[2,512]{1,0:T(2,128)S(1)} %fusion.79, bf16[4992,2,128]{0,2,1:T(8,128)(2,1)} %get-tuple-element.224, s32[]{:T(128)S(6)} %select_n.186, pred[512,1408]{1,0:T(8,128)(4,1)S(1)} %compare_and_fusion.3, bf16[4992,2,192]{0,2,1:T(8,128)(2,1)} %get-tuple-element.227, ...), kind=kOutput, calls=%fused_computation.14.clone.1 | convolution fusion | flops 930089344 | bytes 3184128 | tf_op jit(solution)/shard_map/while/body/eval_jaxpr/hqk,khe->qhe/dot_general | solution.py:97
  136.3 3.7 %fusion.79 = f32[2,512]{1,0:T(2,128)S(1)} fusion(pred[512,1408]{1,0:T(8,128)(4,1)S(1)} %compare_and_fusion.3, bf16[4992,2,192]{0,2,1:T(8,128)(2,1)} %get-tuple-element.227, s32[]{:T(128)S(6)} %select_n.186, bf16[4096,2,192]{0,2,1:T(8,128)(2,1)} %get-tuple-element.226, s32[]{:T(128)S(6)} %select_n.185), kind=kOutput, calls=%fused_computation.85.clone.1 | convolution fusion | flops 559416704 | bytes 2199560 | tf_op jit(solution)/shard_map/while/body/eval_jaxpr/sub | solution.py:95
  140.0 4.4 %fusion.80 = bf16[2,128,512]{2,1,0:T(8,128)(2,1)S(1)} fusion(f32[2,512]{1,0:T(2,128)S(1)} %fusion.79, bf16[4992,2,128]{0,2,1:T(8,128)(2,1)} %get-tuple-element.224, s32[]{:T(128)S(6)} %select_n.186, pred[512,1408]{1,0:T(8,128)(4,1)S(1)} %compare_and_fusion.3, bf16[4992,2,192]{0,2,1:T(8,128)(2,1)} %get-tuple-element.227, ...), kind=kOutput, calls=%fused_computation.14.clone.1 | convolution fusion | flops 930089344 | bytes 3184128 | tf_op jit(solution)/shard_map/while/body/eval_jaxpr/hqk,khe->qhe/dot_general | solution.py:97
  147.2 3.7 %fusion.79 = f32[2,512]{1,0:T(2,128)S(1)} fusion(pred[512,1408]{1,0:T(8,128)(4,1)S(1)} %compare_and_fusion.3, bf16[4992,2,192]{0,2,1:T(8,128)(2,1)} %get-tuple-element.227, s32[]{:T(128)S(6)} %select_n.186, bf16[4096,2,192]{0,2,1:T(8,128)(2,1)} %get-tuple-element.226, s32[]{:T(128)S(6)} %select_n.185), kind=kOutput, calls=%fused_computation.85.clone.1 | convolution fusion | flops 559416704 | bytes 2199560 | tf_op jit(solution)/shard_map/while/body/eval_jaxpr/sub | solution.py:95
  151.0 4.4 %fusion.80 = bf16[2,128,512]{2,1,0:T(8,128)(2,1)S(1)} fusion(f32[2,512]{1,0:T(2,128)S(1)} %fusion.79, bf16[4992,2,128]{0,2,1:T(8,128)(2,1)} %get-tuple-element.224, s32[]{:T(128)S(6)} %select_n.186, pred[512,1408]{1,0:T(8,128)(4,1)S(1)} %compare_and_fusion.3, bf16[4992,2,192]{0,2,1:T(8,128)(2,1)} %get-tuple-element.227, ...), kind=kOutput, calls=%fused_computation.14.clone.1 | convolution fusion | flops 930089344 | bytes 3184128 | tf_op jit(solution)/shard_map/while/body/eval_jaxpr/hqk,khe->qhe/dot_general | solution.py:97
  158.2 3.7 %fusion.79 = f32[2,512]{1,0:T(2,128)S(1)} fusion(pred[512,1408]{1,0:T(8,128)(4,1)S(1)} %compare_and_fusion.3, bf16[4992,2,192]{0,2,1:T(8,128)(2,1)} %get-tuple-element.227, s32[]{:T(128)S(6)} %select_n.186, bf16[4096,2,192]{0,2,1:T(8,128)(2,1)} %get-tuple-element.226, s32[]{:T(128)S(6)} %select_n.185), kind=kOutput, calls=%fused_computation.85.clone.1 | convolution fusion | flops 559416704 | bytes 2199560 | tf_op jit(solution)/shard_map/while/body/eval_jaxpr/sub | solution.py:95
  161.9 4.4 %fusion.80 = bf16[2,128,512]{2,1,0:T(8,128)(2,1)S(1)} fusion(f32[2,512]{1,0:T(2,128)S(1)} %fusion.79, bf16[4992,2,128]{0,2,1:T(8,128)(2,1)} %get-tuple-element.224, s32[]{:T(128)S(6)} %select_n.186, pred[512,1408]{1,0:T(8,128)(4,1)S(1)} %compare_and_fusion.3, bf16[4992,2,192]{0,2,1:T(8,128)(2,1)} %get-tuple-element.227, ...), kind=kOutput, calls=%fused_computation.14.clone.1 | convolution fusion | flops 930089344 | bytes 3184128 | tf_op jit(solution)/shard_map/while/body/eval_jaxpr/hqk,khe->qhe/dot_general | solution.py:97
  169.1 3.7 %fusion.79 = f32[2,512]{1,0:T(2,128)S(1)} fusion(pred[512,1408]{1,0:T(8,128)(4,1)S(1)} %compare_and_fusion.3, bf16[4992,2,192]{0,2,1:T(8,128)(2,1)} %get-tuple-element.227, s32[]{:T(128)S(6)} %select_n.186, bf16[4096,2,192]{0,2,1:T(8,128)(2,1)} %get-tuple-element.226, s32[]{:T(128)S(6)} %select_n.185), kind=kOutput, calls=%fused_computation.85.clone.1 | convolution fusion | flops 559416704 | bytes 2199560 | tf_op jit(solution)/shard_map/while/body/eval_jaxpr/sub | solution.py:95
  172.9 4.4 %fusion.80 = bf16[2,128,512]{2,1,0:T(8,128)(2,1)S(1)} fusion(f32[2,512]{1,0:T(2,128)S(1)} %fusion.79, bf16[4992,2,128]{0,2,1:T(8,128)(2,1)} %get-tuple-element.224, s32[]{:T(128)S(6)} %select_n.186, pred[512,1408]{1,0:T(8,128)(4,1)S(1)} %compare_and_fusion.3, bf16[4992,2,192]{0,2,1:T(8,128)(2,1)} %get-tuple-element.227, ...), kind=kOutput, calls=%fused_computation.14.clone.1 | convolution fusion | flops 930089344 | bytes 3184128 | tf_op jit(solution)/shard_map/while/body/eval_jaxpr/hqk,khe->qhe/dot_general | solution.py:97
  180.1 3.7 %fusion.79 = f32[2,512]{1,0:T(2,128)S(1)} fusion(pred[512,1408]{1,0:T(8,128)(4,1)S(1)} %compare_and_fusion.3, bf16[4992,2,192]{0,2,1:T(8,128)(2,1)} %get-tuple-element.227, s32[]{:T(128)S(6)} %select_n.186, bf16[4096,2,192]{0,2,1:T(8,128)(2,1)} %get-tuple-element.226, s32[]{:T(128)S(6)} %select_n.185), kind=kOutput, calls=%fused_computation.85.clone.1 | convolution fusion | flops 559416704 | bytes 2199560 | tf_op jit(solution)/shard_map/while/body/eval_jaxpr/sub | solution.py:95
  183.8 4.4 %fusion.80 = bf16[2,128,512]{2,1,0:T(8,128)(2,1)S(1)} fusion(f32[2,512]{1,0:T(2,128)S(1)} %fusion.79, bf16[4992,2,128]{0,2,1:T(8,128)(2,1)} %get-tuple-element.224, s32[]{:T(128)S(6)} %select_n.186, pred[512,1408]{1,0:T(8,128)(4,1)S(1)} %compare_and_fusion.3, bf16[4992,2,192]{0,2,1:T(8,128)(2,1)} %get-tuple-element.227, ...), kind=kOutput, calls=%fused_computation.14.clone.1 | convolution fusion | flops 930089344 | bytes 3184128 | tf_op jit(solution)/shard_map/while/body/eval_jaxpr/hqk,khe->qhe/dot_general | solution.py:97
  190.8 17.4 %while.14 = (s32[]{:T(128)}, bf16[5120,256]{1,0:T(8,128)(2,1)S(1)}, s32[8,2]{0,1:T(2,128)S(1)}, bf16[8,1024,256]{2,1,0:T(8,128)(2,1)}, s32[]{:T(128)}) while((s32[]{:T(128)}, bf16[5120,256]{1,0:T(8,128)(2,1)S(1)}, s32[8,2]{0,1:T(2,128)S(1)}, bf16[8,1024,256]{2,1,0:T(8,128)(2,1)}, s32[]{:T(128)}) %tuple.41), condition=%wide.while_cond, body=%wide.while_body.sunk | while | flops 2 | bytes 1049689 | solution.py:46
  208.2 8.3 %all-to-all-start.1 = ((bf16[8,1024,256]{2,1,0:T(8,128)(2,1)}), bf16[8,1024,256]{2,1,0:T(8,128)(2,1)}, u32[]{:S(2)}, u32[]{:S(2)}) async-start(bf16[8,1024,256]{2,1,0:T(8,128)(2,1)} %get-tuple-element.102), calls=%async_computation.1 | async-start | bytes 8388608 | tf_op jit(solution)/shard_map/all_to_all | solution.py:139
  219.4 93.9 %all-to-all-done.1 = bf16[8,1024,256]{2,1,0:T(8,128)(2,1)} async-done(((bf16[8,1024,256]{2,1,0:T(8,128)(2,1)}), bf16[8,1024,256]{2,1,0:T(8,128)(2,1)}, u32[]{:S(2)}, u32[]{:S(2)}) %all-to-all-start.1) | async-done | bytes 4194336 | tf_op jit(solution)/shard_map/all_to_all | solution.py:139
  313.3 2.9 gather_fusion.3
  316.5 34.0 %all_to_all.37 = bf16[32,128,256]{2,1,0:T(8,128)(2,1)S(1)} all-to-all(bf16[32,128,256]{2,1,0:T(8,128)(2,1)S(1)} %broadcast_select_fusion), channel_id=1, replica_groups=mesh['dp'=8,'seq'=32] {'seq'}, dimensions={0} | all-to-all | bytes 4194304 | tf_op jit(solution)/shard_map/all_to_all | solution.py:143
  350.5 2.9 copy.35
  353.4 4.1 %copy.36 = bf16[128,8192]{1,0:T(8,128)(2,1)} copy(bf16[128,8192]{0,1:T(8,128)(2,1)} %bitcast.66) | data formatting | bytes 4194304 | tf_op jit(solution)/shard_map/all_to_all | solution.py:143
  (132 shorter events, 45.1 us)
Async XLA Ops:
  6.5 87.4 %copy-start = (bf16[512,512]{1,0:T(8,128)(2,1)S(1)}, bf16[512,512]{1,0:T(8,128)(2,1)}, u32[]{:S(2)}) copy-start(bf16[512,512]{1,0:T(8,128)(2,1)} %param.14) | copy-start | bytes 1572868
  6.5 84.1 %all-gather.2.cloned.1.call-start = ((), (), s32[]{:S(2)}) async-start(), calls=%async_computation.3 | async-start | bytes 4325376 | tf_op jit(solution)/shard_map/all_gather | solution.py:116
  11.9 8.8 %copy-start.1 = (s32[8]{0:T(128)S(1)}, s32[8]{0:T(128)}, u32[]{:S(2)}) copy-start(s32[8]{0:T(128)} %param.15) | copy-start | bytes 100
  11.9 9.9 %copy-start.5 = (s32[8]{0:T(128)S(1)}, s32[8]{0:T(128)}, u32[]{:S(2)}) copy-start(s32[8]{0:T(128)} %param.16) | copy-start | bytes 100
  11.9 10.8 %copy-start.3 = (bf16[128,64]{0,1:T(8,128)(2,1)S(1)}, bf16[128,64]{0,1:T(8,128)(2,1)}, u32[]{:S(2)}) copy-start(bf16[128,64]{0,1:T(8,128)(2,1)} %param.12) | copy-start | bytes 49156
  11.9 67.1 %all-to-all-start = ((bf16[128,32,384]{0,2,1:T(8,128)(2,1)}), bf16[128,32,384]{0,2,1:T(8,128)(2,1)}, u32[]{:S(2)}, u32[]{:S(2)}) async-start(bf16[128,32,384]{0,2,1:T(8,128)(2,1)} %bitcast.64), calls=%async_computation | async-start | bytes 6291456 | tf_op jit(solution)/shard_map/all_to_all | solution.py:114
  84.8 9.1 %copy-start.4 = (f32[512]{0:T(512)S(1)}, f32[512]{0:T(512)}, u32[]{:S(2)}) copy-start(f32[512]{0:T(512)} %param.13) | copy-start | bytes 6148
  90.6 3.4 copy-start.2
  208.2 105.2 %all-to-all-start.1 = ((bf16[8,1024,256]{2,1,0:T(8,128)(2,1)}), bf16[8,1024,256]{2,1,0:T(8,128)(2,1)}, u32[]{:S(2)}, u32[]{:S(2)}) async-start(bf16[8,1024,256]{2,1,0:T(8,128)(2,1)} %get-tuple-element.102), calls=%async_computation.1 | async-start | bytes 8388608 | tf_op jit(solution)/shard_map/all_to_all | solution.py:139
Sparse Core Ops, SparseCore 0:
  9.9 77.9 all-gather.1
where the time goes:
time: 366 us; the launch traced here: 364 us
  waiting for transfers between devices  94.6 us (26%)
  blocking collectives  90.3 us (25%)
  matrix products  67.6 us (18%)
  local copies, waits for them, and re-layouts  62.8 us (17%)
  starting transfers between devices  17.1 us (5%)
  between operations  13.6 us (4%)
  other arithmetic  12.9 us (4%)
  loops' own time  5.5 us (2%)
    all_to_all x1, waiting for transfers between devices, on_device(): lax.all_to_all(pack_slots(local_out, slot_starts, slot_rows), 'dp', split...  93.9 us
    all_gather x1, blocking collectives, on_device(): lax.all_gather(key_rope, 'seq', axis=0, tiled=True)  56.2 us
    dot_general x8, matrix products, scored(): jnp.einsum('hqk,khe->qhe', weights, value_tile, preferred_element_type=jn...  34.9 us
    all_to_all x1, blocking collectives, on_device(): lax.all_to_all(bucketed, 'seq', split_axis=0, concat_axis=1, tiled=True)  34 us
    sub x8, matrix products, scored(): exponent = jnp.exp(scores - row_max)  29.8 us
    gather x24, local copies, waits for them, and re-layouts  17.3 us
    all_to_all x1, starting transfers between devices, on_device(): lax.all_to_all(queries, 'seq', split_axis=1, concat_axis=0, tiled=True)  8.78 us
    all_to_all x1, starting transfers between devices, on_device(): lax.all_to_all(pack_slots(local_out, slot_starts, slot_rows), 'dp', split...  8.3 us
  transfers between devices with their start and end apart: 3, of which 1 were waited for; matrix products, arithmetic and copies ran while one was open for 6% of the time, Pallas kernels for 0%

commit v1 on v0

v1 whole, which is shorter than its diff:
```python
import functools
import math

import jax
import jax.numpy as jnp
from jax import lax
from jax.experimental import pallas as pl
from jax.experimental.pallas import tpu as pltpu
from jax.sharding import PartitionSpec as P

HD_NOPE = 128
HD_ROPE = 64
HD_V = 128
BLK = 128
LAT = 512
NBLK = 32
N_DP = 8
SEG_MOST = 8
NY, NX, NC = 4, 4, 2
N_SEQ = NY * NX * NC
LEAD = (SEG_MOST - 1) * BLK
KEYS = LEAD + 2 * BLK
XW = LAT + 2 * HD_ROPE
EPS = 1e-06
NEG = -1e30
EXP_SCALE = (HD_NOPE + HD_ROPE) ** -0.5 * math.log2(math.e)
HALF = BLK // 2


def seq_peer(y, x, c, o):
    dc, dx, dy = o % NC, (o // NC) % NX, o // (NC * NX)
    return ((y + dy) % NY) * (NX * NC) + ((x + dx) % NX) * NC + (c + dc) % NC


def seq_source(y, x, c, o):
    dc, dx, dy = o % NC, (o // NC) % NX, o // (NC * NX)
    return ((y + NY - dy) % NY) * (NX * NC) + ((x + NX - dx) % NX) * NC + (c + NC - dc) % NC


def kernel(
    queries, latent, rope2, gain, kv_up, seg, bucket_of, breaks,
    out,
    xall, qa, qb, wts, kext, vext, att, zsend, zrecv0, zrecv1, osend,
    starts_sm, first_sm, pick_sm, slot_sm,
    l1_send, l1_recv, l2_send, l2_recv, sib_send, sib_recv,
    q_send, q_recv, z_send, z_recv, o_send, o_recv, own_sem,
):
    s = lax.axis_index("dp")
    me = lax.axis_index("seq")
    y, x, c = me // (NX * NC), (me // NC) % NX, me % NC

    def remote(src, dst, send, recv, **axes):
        return pltpu.make_async_remote_copy(
            src_ref=src, dst_ref=dst, send_sem=send, recv_sem=recv,
            device_id=axes, device_id_type=pl.DeviceIdType.MESH,
        )

    zrecv = (zrecv0, zrecv1)

    barrier = pltpu.get_barrier_semaphore()

    def greet_seq(o, carry):
        pl.semaphore_signal(barrier, inc=1, device_id={"seq": seq_peer(y, x, c, o)},
                            device_id_type=pl.DeviceIdType.MESH)
        return carry

    lax.fori_loop(1, N_SEQ, greet_seq, 0)
    for d in range(1, N_DP):
        pl.semaphore_signal(barrier, inc=1, device_id={"dp": (s + d) % N_DP},
                            device_id_type=pl.DeviceIdType.MESH)

    lat = latent[...].astype(jnp.float32)
    normed = (
        lat * lax.rsqrt(jnp.mean(lat * lat, axis=1, keepdims=True) + EPS) * gain[...]
    ).astype(jnp.bfloat16)
    rows = jnp.concatenate([normed, rope2[...]], axis=1).reshape(2, HALF, XW)
    xall[y, x, c] = rows

    pl.semaphore_wait(barrier, N_SEQ - 1 + N_DP - 1)

    def at_x(d):
        return y * (NX * NC) + ((x + d) % NX) * NC + c

    def at_y(d):
        return ((y + d) % NY) * (NX * NC) + x * NC + c

    sibling = y * (NX * NC) + x * NC + (1 - c)
    ph1 = []
    for d in range(1, 4):
        own_a, own_b = xall.at[y, x, c, 0], xall.at[y, x, c, 1]
        ph1.append(remote(own_a, own_a, l1_send.at[0, d], l1_recv.at[0, d], seq=at_x(d)))
        ph1.append(remote(own_b, own_b, l1_send.at[1, d], l1_recv.at[1, d], seq=at_y(d)))
    for cp in ph1:
        cp.start()

    def q_copy(o, part, peer, slot):
        width = 2 * BLK if part == 0 else BLK
        begin = pl.multiple_of(peer * (3 * BLK) + part * 2 * BLK, BLK)
        dst = (qa if part == 0 else qb).at[slot]
        return remote(queries.at[:, pl.ds(begin, width)], dst,
                      q_send.at[part, o], q_recv.at[part, o], seq=peer)

    def q_start(part, lo, hi):
        def body(o, carry):
            q_copy(o, part, seq_peer(y, x, c, o), me).start()
            return carry
        lax.fori_loop(lo, hi, body, 0)

    def q_arrive(part):
        def body(o, carry):
            q_copy(o, part, seq_peer(y, x, c, o), seq_source(y, x, c, o)).wait_recv()
            return carry
        lax.fori_loop(1, N_SEQ, body, 0)

    def q_drain(part):
        def body(o, carry):
            q_copy(o, part, seq_peer(y, x, c, o), me).wait_send()
            return carry
        lax.fori_loop(1, N_SEQ, body, 0)

    def q_own(part):
        width = 2 * BLK if part == 0 else BLK
        begin = pl.multiple_of(me * (3 * BLK) + part * 2 * BLK, BLK)
        return pltpu.make_async_copy(queries.at[:, pl.ds(begin, width)],
                                     (qa if part == 0 else qb).at[me], own_sem.at[part])

    q_own(0).start()
    q_own(1).start()

    for d in range(1, 4):
        there = xall.at[y, (x + NX - d) % NX, c, 0]
        remote(there, there, l1_send.at[0, d], l1_recv.at[0, d], seq=at_x(d)).wait_recv()
    row_a = xall.at[y, :, c, 0]
    ph2 = [remote(row_a, row_a, l2_send.at[0, d], l2_recv.at[0, d], seq=at_y(d)) for d in range(1, 4)]
    for cp in ph2:
        cp.start()
    for d in range(1, 4):
        there = xall.at[(y + NY - d) % NY, x, c, 1]
        remote(there, there, l1_send.at[1, d], l1_recv.at[1, d], seq=at_y(d)).wait_recv()
    col_b = xall.at[:, x, c, 1]
    ph2b = [remote(col_b, col_b, l2_send.at[1, d], l2_recv.at[1, d], seq=at_x(d)) for d in range(1, 4)]
    for cp in ph2b:
        cp.start()
    sib = [
        remote(row_a, row_a, sib_send.at[0, 0], sib_recv.at[0, 0], seq=sibling),
        remote(col_b, col_b, sib_send.at[1, 0], sib_recv.at[1, 0], seq=sibling),
    ]
    for cp in sib:
        cp.start()

    q_start(0, 1, N_SEQ)
    q_start(1, 1, N_SEQ)

    total = jnp.int32(0)
    start_of = []
    for g in range(N_DP):
        start_of.append(total)
        starts_sm[g] = total
        total = total + seg[g]
    mine = jnp.int32(0)
    for j in range(N_DP):
        mine = mine + jnp.where(bucket_of[j] == s, j, 0)
    for d in range(N_DP):
        b = (s + d) % N_DP
        at = jnp.int32(0)
        for j in range(N_DP):
            at = at + jnp.where(bucket_of[j] == b, j, 0)
        slot_sm[d] = starts_sm[(at - s + N_DP) % N_DP]
    ends, begins = [], []
    total = jnp.int32(0)
    for r in range(N_DP):
        begins.append(total)
        total = total + seg[(mine - r + N_DP) % N_DP]
        ends.append(total)

    def plan_tile(k, first):
        begins_here = breaks[s, k] == 1
        pick = jnp.int32(0)
        for r in range(N_DP):
            begins_here = begins_here | (start_of[r] == k)
            inside = (k >= begins[r]) & (k < ends[r])
            pick = pick + jnp.where(inside, r * SEG_MOST + k - begins[r], 0)
        first = jnp.where(begins_here, k, first)
        first_sm[k] = first
        pick_sm[k] = pick
        return first

    lax.fori_loop(0, NBLK, plan_tile, jnp.int32(0))

    lane = lax.broadcasted_iota(jnp.int32, (LAT, BLK), 1)
    wts[:, : 2 * BLK] = kv_up[:, : 2 * BLK]
    turned = pltpu.roll(kv_up[:, 2 * BLK : 3 * BLK].astype(jnp.float32), HALF, 1)
    wts[:, 2 * BLK : 3 * BLK] = jnp.where(lane < HALF, 0.0, turned).astype(jnp.bfloat16)
    wts[:, 3 * BLK : 4 * BLK] = jnp.where(lane < HALF, turned, 0.0).astype(jnp.bfloat16)
    wts[:, 4 * BLK :] = kv_up[:, 3 * BLK :]
    kext[:, :LEAD, :] = jnp.zeros((2, LEAD, 2 * BLK), jnp.bfloat16)
    vext[:, :LEAD, :] = jnp.zeros((2, LEAD, 2 * BLK), jnp.bfloat16)

    for d in range(1, 4):
        got = xall.at[(y + NY - d) % NY, :, c, 0]
        remote(got, got, l2_send.at[0, d], l2_recv.at[0, d], seq=at_y(d)).wait_recv()
        sib.append(remote(got, got, sib_send.at[0, d], sib_recv.at[0, d], seq=sibling))
        sib[-1].start()
        got = xall.at[:, (x + NX - d) % NX, c, 1]
        remote(got, got, l2_send.at[1, d], l2_recv.at[1, d], seq=at_x(d)).wait_recv()
        sib.append(remote(got, got, sib_send.at[1, d], sib_recv.at[1, d], seq=sibling))
        sib[-1].start()
    for d in range(4):
        got = xall.at[(y + NY - d) % NY, :, 1 - c, 0]
        remote(got, got, sib_send.at[0, d], sib_recv.at[0, d], seq=sibling).wait_recv()
        got = xall.at[:, (x + NX - d) % NX, 1 - c, 1]
        remote(got, got, sib_send.at[1, d], sib_recv.at[1, d], seq=sibling).wait_recv()

    lane2 = lax.broadcasted_iota(jnp.int32, (2 * BLK, BLK), 1)

    def project(i, carry):
        block = xall[i // NX, i % NX].reshape(2 * BLK, XW)
        rot = block[:, LAT:].astype(jnp.float32)
        kv = jnp.dot(block[:, :LAT], wts[...], preferred_element_type=jnp.float32)
        at = pl.ds(pl.multiple_of(LEAD + i * 2 * BLK, BLK), 2 * BLK)
        ones = jnp.ones((2 * BLK, BLK), jnp.bfloat16)
        kext[0, at, :BLK] = kv[:, :BLK].astype(jnp.bfloat16)
        kext[0, at, BLK:] = jnp.where(lane2 < HALF, rot, 0.0).astype(jnp.bfloat16)
        vext[0, at, :BLK] = kv[:, BLK : 2 * BLK].astype(jnp.bfloat16)
        vext[0, at, BLK:] = ones
        kext[1, at, :BLK] = kv[:, 2 * BLK : 3 * BLK].astype(jnp.bfloat16)
        kext[1, at, BLK:] = jnp.where(lane2 < HALF, kv[:, 3 * BLK : 4 * BLK], rot).astype(jnp.bfloat16)
        vext[1, at, :BLK] = kv[:, 4 * BLK :].astype(jnp.bfloat16)
        vext[1, at, BLK:] = ones
        return carry

    lax.fori_loop(0, NBLK // 2, project, 0)

    row_id = lax.broadcasted_iota(jnp.int32, (BLK, BLK), 0)
    col_id = lax.broadcasted_iota(jnp.int32, (BLK, BLK), 1)
    causal = col_id <= row_id

    def attend(h):
        def body(i, carry):
            if h == 0:
                q = qa[pl.ds(2 * i, 2)].reshape(2 * BLK, 2 * BLK)
            else:
                q = jnp.concatenate(
                    [qa[pl.ds(2 * i, 2), :, BLK:], qb[pl.ds(2 * i, 2)]], axis=2
                ).reshape(2 * BLK, 2 * BLK)
            at = pl.ds(pl.multiple_of(i * 2 * BLK, BLK), KEYS)
            sc = lax.dot_general(q, kext[h, at, :], (((1,), (1,)), ((), ())),
                                 preferred_element_type=jnp.float32)
            halves = []
            for half in range(2):
                part = sc[half * BLK : (half + 1) * BLK]
                low = first_sm[2 * i + half] - (2 * i - (SEG_MOST - 1))
                tiles = []
                for u in range(half, half + SEG_MOST):
                    tile = part[:, u * BLK : (u + 1) * BLK]
                    ok = causal if u == half + SEG_MOST - 1 else (low <= u)
                    tiles.append(jnp.where(ok, tile, NEG))
                top = functools.reduce(jnp.maximum, tiles)
                top = jnp.max(top, axis=1, keepdims=True)
                w = [jnp.exp2((t - top) * EXP_SCALE).astype(jnp.bfloat16) for t in tiles]
                none = jnp.zeros((BLK, BLK), jnp.bfloat16)
                halves.append(jnp.concatenate(w + [none] if half == 0 else [none] + w, axis=1))
            o = jnp.dot(jnp.concatenate(halves, axis=0), vext[h, at, :],
                        preferred_element_type=jnp.float32)
            o = (o[:, :BLK] / o[:, BLK:]).astype(jnp.bfloat16)
            att[h, pl.ds(2 * i, 2)] = o.reshape(2, BLK, BLK)
            return carry

        lax.fori_loop(0, NBLK // 2, body, 0)

    def z_copy(h, d, slot):
        return remote(zsend.at[h, d], zrecv[h].at[slot], z_send.at[h, d], z_recv.at[h, d],
                      dp=(s + d) % N_DP)

    def send_dp(h):
        for d in list(range(1, N_DP)) + [0]:
            base = slot_sm[d]
            for j in range(SEG_MOST):
                tile = att[h, jnp.minimum(base + j, NBLK - 1)]
                if d == 0:
                    zrecv[h][s, j] = tile
                else:
                    zsend[h, d, j] = tile
            if d:
                z_copy(h, d, s).start()

    def o_copy(h, o, owner, peer):
        begin = pl.multiple_of((2 * owner + h) * BLK, BLK)
        return remote(osend.at[h, o], out.at[:, pl.ds(begin, BLK)], o_send.at[h, o], o_recv.at[h, o],
                      seq=peer)

    def o_own(h):
        begin = pl.multiple_of((2 * me + h) * BLK, BLK)
        return pltpu.make_async_copy(osend.at[h, 0], out.at[:, pl.ds(begin, BLK)], own_sem.at[2 + h])

    def send_seq(h):
        for d in range(1, N_DP):
            z_copy(h, d, (s + N_DP - d) % N_DP).wait_recv()

        def body(o, carry):
            peer = seq_peer(y, x, c, o)
            pick = pick_sm[peer]
            osend[h, o] = zrecv[h][pick // SEG_MOST, pick % SEG_MOST]
            o_copy(h, o, me, peer).start()
            return carry

        lax.fori_loop(1, N_SEQ, body, 0)
        pick = pick_sm[me]
        osend[h, 0] = zrecv[h][pick // SEG_MOST, pick % SEG_MOST]
        o_own(h).start()

    q_own(0).wait()
    q_own(1).wait()
    q_arrive(0)
    attend(0)
    send_dp(0)
    q_arrive(1)
    attend(1)
    send_dp(1)
    send_seq(0)
    send_seq(1)

    for cp in ph1 + ph2 + ph2b + sib:
        cp.wait_send()
    q_drain(0)
    q_drain(1)
    for h in range(2):
        for d in range(1, N_DP):
            z_copy(h, d, s).wait_send()
        o_own(h).wait()

        def body(o, carry):
            cp = o_copy(h, o, seq_source(y, x, c, o), seq_peer(y, x, c, o))
            cp.wait_send()
            cp.wait_recv()
            return carry

        lax.fori_loop(1, N_SEQ, body, 0)


def on_device(queries, kv_latent, key_rope, kv_gain, kv_up, segment_blocks, bucket_of, doc_breaks):
    bf16 = jnp.bfloat16
    rope2 = jnp.concatenate([key_rope, key_rope], axis=1)
    vmem = pl.BlockSpec(memory_space=pltpu.VMEM)
    smem = pl.BlockSpec(memory_space=pltpu.SMEM)
    anywhere = pl.BlockSpec(memory_space=pl.ANY)
    dma = pltpu.SemaphoreType.DMA
    return pl.pallas_call(
        kernel,
        out_shape=jax.ShapeDtypeStruct((BLK, N_SEQ * 2 * HD_V), bf16),
        in_specs=[anywhere, vmem, vmem, vmem, vmem, smem, smem, smem],
        out_specs=anywhere,
        scratch_shapes=[
            pltpu.VMEM((NY, NX, NC, 2, HALF, XW), bf16),
            pltpu.VMEM((NBLK, BLK, 2 * BLK), bf16),
            pltpu.VMEM((NBLK, BLK, BLK), bf16),
            pltpu.VMEM((LAT, 5 * BLK), bf16),
            pltpu.VMEM((2, LEAD + NBLK * BLK, 2 * BLK), bf16),
            pltpu.VMEM((2, LEAD + NBLK * BLK, 2 * BLK), bf16),
            pltpu.VMEM((2, NBLK, BLK, BLK), bf16),
            pltpu.VMEM((2, N_DP, SEG_MOST, BLK, BLK), bf16),
            pltpu.VMEM((N_DP, SEG_MOST, BLK, BLK), bf16),
            pltpu.VMEM((N_DP, SEG_MOST, BLK, BLK), bf16),
            pltpu.VMEM((2, N_SEQ, BLK, BLK), bf16),
            pltpu.SMEM((N_DP,), jnp.int32),
            pltpu.SMEM((NBLK,), jnp.int32),
            pltpu.SMEM((NBLK,), jnp.int32),
            pltpu.SMEM((N_DP,), jnp.int32),
            dma((2, 4)), dma((2, 4)), dma((2, 4)), dma((2, 4)), dma((2, 4)), dma((2, 4)),
            dma((2, N_SEQ)), dma((2, N_SEQ)),
            dma((2, N_DP)), dma((2, N_DP)),
            dma((2, N_SEQ)), dma((2, N_SEQ)),
            dma((4,)),
        ],
        compiler_params=pltpu.CompilerParams(
            collective_id=0, has_side_effects=True, vmem_limit_bytes=56 * 2**20
        ),
    )(queries, kv_latent, rope2, kv_gain.reshape(1, LAT), kv_up, segment_blocks, bucket_of, doc_breaks)


def solution(mesh):
    in_specs = (
        P(("dp", "seq"), None),
        P(("dp", "seq"), None),
        P(("dp", "seq"), None),
        P(),
        P(None, "seq"),
        P(),
        P(),
        P(),
    )
    return jax.shard_map(
        on_device, mesh=mesh, in_specs=in_specs, out_specs=P(("dp", "seq"), None), check_vma=False
    )
```

time: 366 us -> 200 us (0.55)
  Pallas kernels: 0 us -> 195 us
  waiting for transfers between devices: 94.6 us -> 0 us
  blocking collectives: 90.3 us -> 0 us
  matrix products: 67.6 us -> 0 us
  local copies, waits for them, and re-layouts: 62.8 us -> 3.92 us
  starting transfers between devices: 17.1 us -> 0 us
  between operations: 13.6 us -> 0.01 us
  other arithmetic: 12.9 us -> 0.71 us
  loops' own time: 5.5 us -> 0 us
    pallas_call x0 -> x1, Pallas kernels: none -> 195 us  [on_device(): pl.pallas_call(kernel, out_shape=jax.ShapeDtypeStruct((BLK, N_SEQ * 2 * H...]
    all_to_all x2 -> x0, waiting for transfers between devices: 93.9 us -> none  [the longest x1 93.9 us: on_device(): lax.all_to_all(pack_slots(local_out, slot_starts, slot_rows), 'dp', split...]
    all_gather x1 -> x0, blocking collectives: 56.2 us -> none  [on_device(): lax.all_gather(key_rope, 'seq', axis=0, tiled=True)]
    dot_general x9 -> x0, matrix products: 37.8 us -> none  [the longest x8 34.9 us: scored(): jnp.einsum('hqk,khe->qhe', weights, value_tile, preferred_element_type=jn...]
    all_to_all x1 -> x0, blocking collectives: 34 us -> none  [on_device(): lax.all_to_all(bucketed, 'seq', split_axis=0, concat_axis=1, tiled=True)]
    sub x8 -> x0, matrix products: 29.8 us -> none  [scored(): exponent = jnp.exp(scores - row_max)]
    gather x28 -> x0, local copies, waits for them, and re-layouts: 22.2 us -> none
    all_to_all x2 -> x0, starting transfers between devices: 17.1 us -> none  [the longest x1 8.78 us: on_device(): lax.all_to_all(queries, 'seq', split_axis=1, concat_axis=0, tiled=True)]
  transfers between devices with their start and end apart: 3 -> 0, of which waited for: 1 -> 0; matrix products, arithmetic and copies ran while one was open for 6% -> 0% of each run, Pallas kernels for 0% -> 0%
where the time goes in v1:
time: 200 us
  Pallas kernels  195 us (98%)
  local copies, waits for them, and re-layouts  3.92 us (2%)
    pallas_call x1, Pallas kernels, on_device(): pl.pallas_call(kernel, out_shape=jax.ShapeDtypeStruct((BLK, N_SEQ * 2 * H...  195 us

profile of v1, /device:TPU:1, one launch (start us, length us, event | category | flops | bytes accessed | tf_op | source)
XLA Modules:
  0.0 199.7 jit_solution(15533563011686998285)
XLA Ops:
  0.0 0.8 copy.9
  0.8 0.7 pad_maximum_fusion.rope2
  1.5 195.0 %shard_map.82 = bf16[128,8192]{1,0:T(8,128)(2,1)} custom-call(bf16[128,12288]{1,0:T(8,128)(2,1)} %queries.1, bf16[128,512]{1,0:T(8,128)(2,1)} %latent.1, bf16[128,128]{1,0:T(8,128)(2,1)} %pad_maximum_fusion.rope2, f32[1,512]{1,0:T(1,128)} %bitcast.1, bf16[512,512]{1,0:T(8,128)(2,1)} %kv_up.1, s32[8]{0:T(128)} %seg.1, s32[8]{0:T(128)} %bucket_of.1, ...), custom_call_target="tpu_custom_call" | custom-call | tf_op jit(solution)/shard_map/pallas_call | solution.py:348
  196.6 3.1 %copy.12 = bf16[128,8192]{1,0:T(8,128)(2,1)} copy(bf16[128,8192]{1,0:T(8,128)(2,1)} %shard_map.82) | data formatting | bytes 4194304

commit v2 on v1

--- a/solution.py
+++ b/solution.py
@@ -19,8 +19,12 @@
 NY, NX, NC = 4, 4, 2
 N_SEQ = NY * NX * NC
 LEAD = (SEG_MOST - 1) * BLK
-KEYS = LEAD + 2 * BLK
+GROUP = 4
+KEYS = LEAD + GROUP * BLK
 XW = LAT + 2 * HD_ROPE
+ROUNDS = 4
+ORDER = (20, 21, 12, 24, 13, 25, 18, 6, 19, 7, 22, 2, 23, 3, 28, 8, 29, 9, 4, 16, 5, 17, 10, 30, 11, 31, 14, 26, 15, 27, 1)
+Z_ORDER = (4, 3, 5, 2, 6, 1, 7, 0)
 EPS = 1e-06
 NEG = -1e30
 EXP_SCALE = (HD_NOPE + HD_ROPE) ** -0.5 * math.log2(math.e)
@@ -40,7 +44,7 @@
 def kernel(
     queries, latent, rope2, gain, kv_up, seg, bucket_of, breaks,
     out,
-    xall, qa, qb, wts, kext, vext, att, zsend, zrecv0, zrecv1, osend,
+    xall, qa, qb, wts, kext, vext, att, zsend, zrecv0, zrecv1, zrecv2, zrecv3, osend,
     starts_sm, first_sm, pick_sm, slot_sm,
     l1_send, l1_recv, l2_send, l2_recv, sib_send, sib_recv,
     q_send, q_recv, z_send, z_recv, o_send, o_recv, own_sem,
@@ -55,7 +59,7 @@
             device_id=axes, device_id_type=pl.DeviceIdType.MESH,
         )
 
-    zrecv = (zrecv0, zrecv1)
+    zrecv = (zrecv0, zrecv1, zrecv2, zrecv3)
 
     barrier = pltpu.get_barrier_semaphore()
 
@@ -93,39 +97,41 @@
     for cp in ph1:
         cp.start()
 
-    def q_copy(o, part, peer, slot):
-        width = 2 * BLK if part == 0 else BLK
-        begin = pl.multiple_of(peer * (3 * BLK) + part * 2 * BLK, BLK)
-        dst = (qa if part == 0 else qb).at[slot]
-        return remote(queries.at[:, pl.ds(begin, width)], dst,
-                      q_send.at[part, o], q_recv.at[part, o], seq=peer)
-
-    def q_start(part, lo, hi):
+    def q_copy(r, o, peer, slot):
+        h, half = r // 2, r % 2
+        width = BLK if h else 2 * BLK
+        begin = pl.multiple_of(peer * (3 * BLK) + h * 2 * BLK, BLK)
+        return remote(queries.at[pl.ds(half * HALF, HALF), pl.ds(begin, width)],
+                      (qb if h else qa).at[half, slot], q_send.at[r, o], q_recv.at[r, o], seq=peer)
+
+    def q_start(r):
+        for o in ORDER:
+            q_copy(r, o, seq_peer(y, x, c, o), me).start()
+
+    def q_arrive(r):
+        q_own(r).wait()
+
         def body(o, carry):
-            q_copy(o, part, seq_peer(y, x, c, o), me).start()
-            return carry
-        lax.fori_loop(lo, hi, body, 0)
-
-    def q_arrive(part):
-        def body(o, carry):
-            q_copy(o, part, seq_peer(y, x, c, o), seq_source(y, x, c, o)).wait_recv()
+            q_copy(r, o, seq_peer(y, x, c, o), seq_source(y, x, c, o)).wait_recv()
             return carry
         lax.fori_loop(1, N_SEQ, body, 0)
 
-    def q_drain(part):
+    def q_drain(r):
         def body(o, carry):
-            q_copy(o, part, seq_peer(y, x, c, o), me).wait_send()
+            q_copy(r, o, seq_peer(y, x, c, o), me).wait_send()
             return carry
         lax.fori_loop(1, N_SEQ, body, 0)
 
-    def q_own(part):
-        width = 2 * BLK if part == 0 else BLK
-        begin = pl.multiple_of(me * (3 * BLK) + part * 2 * BLK, BLK)
-        return pltpu.make_async_copy(queries.at[:, pl.ds(begin, width)],
-                                     (qa if part == 0 else qb).at[me], own_sem.at[part])
-
-    q_own(0).start()
-    q_own(1).start()
+    def q_own(r):
+        h, half = r // 2, r % 2
+        width = BLK if h else 2 * BLK
+        begin = pl.multiple_of(me * (3 * BLK) + h * 2 * BLK, BLK)
+        return pltpu.make_async_copy(queries.at[pl.ds(half * HALF, HALF), pl.ds(begin, width)],
+                                     (qb if h else qa).at[half, me], own_sem.at[r])
+
+    q_start(0)
+    for r in range(ROUNDS):
+        q_own(r).start()
 
     for d in range(1, 4):
         there = xall.at[y, (x + NX - d) % NX, c, 0]
@@ -148,8 +154,7 @@
     for cp in sib:
         cp.start()
 
-    q_start(0, 1, N_SEQ)
-    q_start(1, 1, N_SEQ)
+    q_start(1)
 
     total = jnp.int32(0)
     start_of = []
@@ -230,107 +235,102 @@
         return carry
 
     lax.fori_loop(0, NBLK // 2, project, 0)
-
-    row_id = lax.broadcasted_iota(jnp.int32, (BLK, BLK), 0)
-    col_id = lax.broadcasted_iota(jnp.int32, (BLK, BLK), 1)
-    causal = col_id <= row_id
-
-    def attend(h):
+    q_start(2)
+    q_start(3)
+
+    row_id = lax.broadcasted_iota(jnp.int32, (HALF, BLK), 0)
+    col_id = lax.broadcasted_iota(jnp.int32, (HALF, BLK), 1)
+    none = jnp.zeros((HALF, BLK), jnp.bfloat16)
+
+    def attend(r):
+        h, half = r // 2, r % 2
+        causal = col_id <= row_id + half * HALF
+
         def body(i, carry):
+            of = pl.ds(GROUP * i, GROUP)
             if h == 0:
-                q = qa[pl.ds(2 * i, 2)].reshape(2 * BLK, 2 * BLK)
+                q = qa[half, of]
             else:
-                q = jnp.concatenate(
-                    [qa[pl.ds(2 * i, 2), :, BLK:], qb[pl.ds(2 * i, 2)]], axis=2
-                ).reshape(2 * BLK, 2 * BLK)
-            at = pl.ds(pl.multiple_of(i * 2 * BLK, BLK), KEYS)
-            sc = lax.dot_general(q, kext[h, at, :], (((1,), (1,)), ((), ())),
-                                 preferred_element_type=jnp.float32)
-            halves = []
-            for half in range(2):
-                part = sc[half * BLK : (half + 1) * BLK]
-                low = first_sm[2 * i + half] - (2 * i - (SEG_MOST - 1))
+                q = jnp.concatenate([qa[half, of, :, BLK:], qb[half, of]], axis=2)
+            at = pl.ds(pl.multiple_of(i * GROUP * BLK, BLK), KEYS)
+            sc = lax.dot_general(q.reshape(GROUP * HALF, 2 * BLK), kext[h, at, :],
+                                 (((1,), (1,)), ((), ())), preferred_element_type=jnp.float32)
+            parts = []
+            for t in range(GROUP):
+                part = sc[t * HALF : (t + 1) * HALF]
+                low = first_sm[GROUP * i + t] - (GROUP * i - (SEG_MOST - 1))
                 tiles = []
-                for u in range(half, half + SEG_MOST):
+                for u in range(t, t + SEG_MOST):
                     tile = part[:, u * BLK : (u + 1) * BLK]
-                    ok = causal if u == half + SEG_MOST - 1 else (low <= u)
+                    ok = causal if u == t + SEG_MOST - 1 else (low <= u)
                     tiles.append(jnp.where(ok, tile, NEG))
                 top = functools.reduce(jnp.maximum, tiles)
                 top = jnp.max(top, axis=1, keepdims=True)
-                w = [jnp.exp2((t - top) * EXP_SCALE).astype(jnp.bfloat16) for t in tiles]
-                none = jnp.zeros((BLK, BLK), jnp.bfloat16)
-                halves.append(jnp.concatenate(w + [none] if half == 0 else [none] + w, axis=1))
-            o = jnp.dot(jnp.concatenate(halves, axis=0), vext[h, at, :],
+                w = [jnp.exp2((e - top) * EXP_SCALE).astype(jnp.bfloat16) for e in tiles]
+                parts.append(jnp.concatenate([none] * t + w + [none] * (GROUP - 1 - t), axis=1))
+            o = jnp.dot(jnp.concatenate(parts, axis=0), vext[h, at, :],
                         preferred_element_type=jnp.float32)
             o = (o[:, :BLK] / o[:, BLK:]).astype(jnp.bfloat16)
-            att[h, pl.ds(2 * i, 2)] = o.reshape(2, BLK, BLK)
+            att[of] = o.reshape(GROUP, HALF, BLK)
             return carry
 
-        lax.fori_loop(0, NBLK // 2, body, 0)
-
-    def z_copy(h, d, slot):
-        return remote(zsend.at[h, d], zrecv[h].at[slot], z_send.at[h, d], z_recv.at[h, d],
+        lax.fori_loop(0, NBLK // GROUP, body, 0, unroll=2)
+
+    def z_copy(r, d, slot):
+        return remote(zsend.at[r, d], zrecv[r].at[slot], z_send.at[r, d], z_recv.at[r, d],
                       dp=(s + d) % N_DP)
 
-    def send_dp(h):
-        for d in list(range(1, N_DP)) + [0]:
+    def send_dp(r):
+        for d in Z_ORDER:
             base = slot_sm[d]
             for j in range(SEG_MOST):
-                tile = att[h, jnp.minimum(base + j, NBLK - 1)]
+                tile = att[jnp.minimum(base + j, NBLK - 1)]
                 if d == 0:
-                    zrecv[h][s, j] = tile
+                    zrecv[r][s, j] = tile
                 else:
-                    zsend[h, d, j] = tile
+                    zsend[r, d, j] = tile
             if d:
-                z_copy(h, d, s).start()
-
-    def o_copy(h, o, owner, peer):
-        begin = pl.multiple_of((2 * owner + h) * BLK, BLK)
-        return remote(osend.at[h, o], out.at[:, pl.ds(begin, BLK)], o_send.at[h, o], o_recv.at[h, o],
-                      seq=peer)
-
-    def o_own(h):
-        begin = pl.multiple_of((2 * me + h) * BLK, BLK)
-        return pltpu.make_async_copy(osend.at[h, 0], out.at[:, pl.ds(begin, BLK)], own_sem.at[2 + h])
-
-    def send_seq(h):
+                z_copy(r, d, s).start()
+
+    def o_part(r, owner):
+        begin = pl.multiple_of((2 * owner + r // 2) * BLK, BLK)
+        return out.at[pl.ds(r % 2 * HALF, HALF), pl.ds(begin, BLK)]
+
+    def o_copy(r, o, owner, peer):
+        return remote(osend.at[r, o], o_part(r, owner), o_send.at[r, o], o_recv.at[r, o], seq=peer)
+
+    def o_own(r):
+        return pltpu.make_async_copy(osend.at[r, 0], o_part(r, me), own_sem.at[ROUNDS + r])
+
+    def send_seq(r):
         for d in range(1, N_DP):
-            z_copy(h, d, (s + N_DP - d) % N_DP).wait_recv()
-
-        def body(o, carry):
+            z_copy(r, d, (s + N_DP - d) % N_DP).wait_recv()
+        for o in ORDER:
             peer = seq_peer(y, x, c, o)
             pick = pick_sm[peer]
-            osend[h, o] = zrecv[h][pick // SEG_MOST, pick % SEG_MOST]
-            o_copy(h, o, me, peer).start()
-            return carry
-
-        lax.fori_loop(1, N_SEQ, body, 0)
+            osend[r, o] = zrecv[r][pick // SEG_MOST, pick % SEG_MOST]
+            o_copy(r, o, me, peer).start()
         pick = pick_sm[me]
-        osend[h, 0] = zrecv[h][pick // SEG_MOST, pick % SEG_MOST]
-        o_own(h).start()
-
-    q_own(0).wait()
-    q_own(1).wait()
-    q_arrive(0)
-    attend(0)
-    send_dp(0)
-    q_arrive(1)
-    attend(1)
-    send_dp(1)
-    send_seq(0)
-    send_seq(1)
+        osend[r, 0] = zrecv[r][pick // SEG_MOST, pick % SEG_MOST]
+        o_own(r).start()
+
+    for r in range(ROUNDS):
+        q_arrive(r)
+        attend(r)
+        send_dp(r)
+    for r in range(ROUNDS):
+        send_seq(r)
 
     for cp in ph1 + ph2 + ph2b + sib:
         cp.wait_send()
-    q_drain(0)
-    q_drain(1)
-    for h in range(2):
+    for r in range(ROUNDS):
+        q_drain(r)
         for d in range(1, N_DP):
-            z_copy(h, d, s).wait_send()
-        o_own(h).wait()
+            z_copy(r, d, s).wait_send()
+        o_own(r).wait()
 
         def body(o, carry):
-            cp = o_copy(h, o, seq_source(y, x, c, o), seq_peer(y, x, c, o))
+            cp = o_copy(r, o, seq_source(y, x, c, o), seq_peer(y, x, c, o))
             cp.wait_send()
             cp.wait_recv()
             return carry
@@ -352,25 +352,24 @@
         out_specs=anywhere,
         scratch_shapes=[
             pltpu.VMEM((NY, NX, NC, 2, HALF, XW), bf16),
-            pltpu.VMEM((NBLK, BLK, 2 * BLK), bf16),
-            pltpu.VMEM((NBLK, BLK, BLK), bf16),
+            pltpu.VMEM((2, NBLK, HALF, 2 * BLK), bf16),
+            pltpu.VMEM((2, NBLK, HALF, BLK), bf16),
             pltpu.VMEM((LAT, 5 * BLK), bf16),
             pltpu.VMEM((2, LEAD + NBLK * BLK, 2 * BLK), bf16),
             pltpu.VMEM((2, LEAD + NBLK * BLK, 2 * BLK), bf16),
-            pltpu.VMEM((2, NBLK, BLK, BLK), bf16),
-            pltpu.VMEM((2, N_DP, SEG_MOST, BLK, BLK), bf16),
-            pltpu.VMEM((N_DP, SEG_MOST, BLK, BLK), bf16),
-            pltpu.VMEM((N_DP, SEG_MOST, BLK, BLK), bf16),
-            pltpu.VMEM((2, N_SEQ, BLK, BLK), bf16),
+            pltpu.VMEM((NBLK, HALF, BLK), bf16),
+            pltpu.VMEM((ROUNDS, N_DP, SEG_MOST, HALF, BLK), bf16),
+            *[pltpu.VMEM((N_DP, SEG_MOST, HALF, BLK), bf16)] * ROUNDS,
+            pltpu.VMEM((ROUNDS, N_SEQ, HALF, BLK), bf16),
             pltpu.SMEM((N_DP,), jnp.int32),
             pltpu.SMEM((NBLK,), jnp.int32),
             pltpu.SMEM((NBLK,), jnp.int32),
             pltpu.SMEM((N_DP,), jnp.int32),
             dma((2, 4)), dma((2, 4)), dma((2, 4)), dma((2, 4)), dma((2, 4)), dma((2, 4)),
-            dma((2, N_SEQ)), dma((2, N_SEQ)),
-            dma((2, N_DP)), dma((2, N_DP)),
-            dma((2, N_SEQ)), dma((2, N_SEQ)),
-            dma((4,)),
+            dma((ROUNDS, N_SEQ)), dma((ROUNDS, N_SEQ)),
+            dma((ROUNDS, N_DP)), dma((ROUNDS, N_DP)),
+            dma((ROUNDS, N_SEQ)), dma((ROUNDS, N_SEQ)),
+            dma((2 * ROUNDS,)),
         ],
         compiler_params=pltpu.CompilerParams(
             collective_id=0, has_side_effects=True, vmem_limit_bytes=56 * 2**20

time: 200 us -> 173 us (0.86)
  Pallas kernels: 195 us -> 168 us
    pallas_call x1, Pallas kernels: 195 us -> 168 us  [on_device(): pl.pallas_call(kernel, out_shape=jax.ShapeDtypeStruct((BLK, N_SEQ * 2 * H...]
where the time goes in v2:
time: 173 us
  Pallas kernels  168 us (97%)
  local copies, waits for them, and re-layouts  3.92 us (2%)
    pallas_call x1, Pallas kernels, on_device(): pl.pallas_call(kernel, out_shape=jax.ShapeDtypeStruct((BLK, N_SEQ * 2 * H...  168 us
    unnamed x2, local copies, waits for them, and re-layouts  3.92 us

profile of v2, /device:TPU:1, one launch (start us, length us, event | category | flops | bytes accessed | tf_op | source)
XLA Modules:
  0.0 173.1 jit_solution(13852832798049027460)
XLA Ops:
  0.0 0.8 copy.9
  0.8 0.7 pad_maximum_fusion.rope2
  1.5 168.4 %shard_map.82 = bf16[128,8192]{1,0:T(8,128)(2,1)} custom-call(bf16[128,12288]{1,0:T(8,128)(2,1)} %queries.1, bf16[128,512]{1,0:T(8,128)(2,1)} %latent.1, bf16[128,128]{1,0:T(8,128)(2,1)} %pad_maximum_fusion.rope2, f32[1,512]{1,0:T(1,128)} %bitcast.1, bf16[512,512]{1,0:T(8,128)(2,1)} %kv_up.1, s32[8]{0:T(128)} %seg.1, s32[8]{0:T(128)} %bucket_of.1, ...), custom_call_target="tpu_custom_call" | custom-call | tf_op jit(solution)/shard_map/pallas_call | solution.py:348
  170.0 3.1 %copy.12 = bf16[128,8192]{1,0:T(8,128)(2,1)} copy(bf16[128,8192]{1,0:T(8,128)(2,1)} %shard_map.82) | data formatting | bytes 4194304

commit v3 on v2

--- a/solution.py
+++ b/solution.py
@@ -12,6 +12,7 @@
 HD_ROPE = 64
 HD_V = 128
 BLK = 128
+HALF = BLK // 2
 LAT = 512
 NBLK = 32
 N_DP = 8
@@ -25,10 +26,13 @@
 ROUNDS = 4
 ORDER = (20, 21, 12, 24, 13, 25, 18, 6, 19, 7, 22, 2, 23, 3, 28, 8, 29, 9, 4, 16, 5, 17, 10, 30, 11, 31, 14, 26, 15, 27, 1)
 Z_ORDER = (4, 3, 5, 2, 6, 1, 7, 0)
+EARLY = 10
+DIRECT = 4
+RELAYED = 12
+PIECE = HALF + (RELAYED - N_DP) * HALF // N_DP
 EPS = 1e-06
 NEG = -1e30
 EXP_SCALE = (HD_NOPE + HD_ROPE) ** -0.5 * math.log2(math.e)
-HALF = BLK // 2
 
 
 def seq_peer(y, x, c, o):
@@ -44,10 +48,10 @@
 def kernel(
     queries, latent, rope2, gain, kv_up, seg, bucket_of, breaks,
     out,
-    xall, qa, qb, wts, kext, vext, att, zsend, zrecv0, zrecv1, zrecv2, zrecv3, osend,
-    starts_sm, first_sm, pick_sm, slot_sm,
+    xa0, xa1, xa2, xa3, xb0, xb1, xb2, xb3, qa, qb, wts, kext, vext, att, zsend, zrecv0, zrecv1, zrecv2, zrecv3, rsend, rrecv0, rrecv1, rrecv2, rrecv3, fsend, osend,
+    starts_sm, first_sm, pick_sm, slot_sm, over_sm, tile_sm, seg_sm, inv_sm,
     l1_send, l1_recv, l2_send, l2_recv, sib_send, sib_recv,
-    q_send, q_recv, z_send, z_recv, o_send, o_recv, own_sem,
+    q_send, q_recv, z_send, z_recv, r_send, r_recv, f_send, f_recv, o_send, o_recv, own_sem,
 ):
     s = lax.axis_index("dp")
     me = lax.axis_index("seq")
@@ -59,7 +63,9 @@
             device_id=axes, device_id_type=pl.DeviceIdType.MESH,
         )
 
+    xa, xb = (xa0, xa1, xa2, xa3), (xb0, xb1, xb2, xb3)
     zrecv = (zrecv0, zrecv1, zrecv2, zrecv3)
+    rrecv = (rrecv0, rrecv1, rrecv2, rrecv3)
 
     barrier = pltpu.get_barrier_semaphore()
 
@@ -77,8 +83,9 @@
     normed = (
         lat * lax.rsqrt(jnp.mean(lat * lat, axis=1, keepdims=True) + EPS) * gain[...]
     ).astype(jnp.bfloat16)
-    rows = jnp.concatenate([normed, rope2[...]], axis=1).reshape(2, HALF, XW)
-    xall[y, x, c] = rows
+    rows = jnp.concatenate([normed, rope2[...]], axis=1)
+    xa0[x, c] = rows[:HALF]
+    xb0[y, c] = rows[HALF:]
 
     pl.semaphore_wait(barrier, N_SEQ - 1 + N_DP - 1)
 
@@ -91,7 +98,7 @@
     sibling = y * (NX * NC) + x * NC + (1 - c)
     ph1 = []
     for d in range(1, 4):
-        own_a, own_b = xall.at[y, x, c, 0], xall.at[y, x, c, 1]
+        own_a, own_b = xa0.at[x, c], xb0.at[y, c]
         ph1.append(remote(own_a, own_a, l1_send.at[0, d], l1_recv.at[0, d], seq=at_x(d)))
         ph1.append(remote(own_b, own_b, l1_send.at[1, d], l1_recv.at[1, d], seq=at_y(d)))
     for cp in ph1:
@@ -104,8 +111,8 @@
         return remote(queries.at[pl.ds(half * HALF, HALF), pl.ds(begin, width)],
                       (qb if h else qa).at[half, slot], q_send.at[r, o], q_recv.at[r, o], seq=peer)
 
-    def q_start(r):
-        for o in ORDER:
+    def q_start(r, order=ORDER):
+        for o in order:
             q_copy(r, o, seq_peer(y, x, c, o), me).start()
 
     def q_arrive(r):
@@ -129,22 +136,22 @@
         return pltpu.make_async_copy(queries.at[pl.ds(half * HALF, HALF), pl.ds(begin, width)],
                                      (qb if h else qa).at[half, me], own_sem.at[r])
 
-    q_start(0)
+    q_start(0, ORDER[:EARLY])
     for r in range(ROUNDS):
         q_own(r).start()
 
     for d in range(1, 4):
-        there = xall.at[y, (x + NX - d) % NX, c, 0]
+        there = xa0.at[(x + NX - d) % NX, c]
         remote(there, there, l1_send.at[0, d], l1_recv.at[0, d], seq=at_x(d)).wait_recv()
-    row_a = xall.at[y, :, c, 0]
-    ph2 = [remote(row_a, row_a, l2_send.at[0, d], l2_recv.at[0, d], seq=at_y(d)) for d in range(1, 4)]
+    row_a = xa0.at[:, c]
+    ph2 = [remote(row_a, xa[d].at[:, c], l2_send.at[0, d], l2_recv.at[0, d], seq=at_y(d)) for d in range(1, 4)]
     for cp in ph2:
         cp.start()
     for d in range(1, 4):
-        there = xall.at[(y + NY - d) % NY, x, c, 1]
+        there = xb0.at[(y + NY - d) % NY, c]
         remote(there, there, l1_send.at[1, d], l1_recv.at[1, d], seq=at_y(d)).wait_recv()
-    col_b = xall.at[:, x, c, 1]
-    ph2b = [remote(col_b, col_b, l2_send.at[1, d], l2_recv.at[1, d], seq=at_x(d)) for d in range(1, 4)]
+    col_b = xb0.at[:, c]
+    ph2b = [remote(col_b, xb[d].at[:, c], l2_send.at[1, d], l2_recv.at[1, d], seq=at_x(d)) for d in range(1, 4)]
     for cp in ph2b:
         cp.start()
     sib = [
@@ -154,27 +161,45 @@
     for cp in sib:
         cp.start()
 
-    q_start(1)
-
-    total = jnp.int32(0)
-    start_of = []
+    q_start(0, ORDER[EARLY:])
+
+    total, over = jnp.int32(0), jnp.int32(0)
+    start_of, over_of = [], []
     for g in range(N_DP):
         start_of.append(total)
         starts_sm[g] = total
         total = total + seg[g]
+        over_of.append(over)
+        over_sm[g] = over
+        over = over + jnp.maximum(seg[g] - DIRECT, 0)
+    over_of.append(over)
     mine = jnp.int32(0)
-    for j in range(N_DP):
-        mine = mine + jnp.where(bucket_of[j] == s, j, 0)
     for d in range(N_DP):
         b = (s + d) % N_DP
         at = jnp.int32(0)
         for j in range(N_DP):
             at = at + jnp.where(bucket_of[j] == b, j, 0)
+        if d == 0:
+            mine = at
+        inv_sm[d] = at
         slot_sm[d] = starts_sm[(at - s + N_DP) % N_DP]
-    ends, begins = [], []
+
+    def plan_over(k, carry):
+        tile, of = jnp.int32(0), jnp.int32(0)
+        for g in range(N_DP):
+            inside = (k >= over_of[g]) & (k < over_of[g + 1])
+            tile = tile + jnp.where(inside, start_of[g] + DIRECT + k - over_of[g], 0)
+            of = of + jnp.where(inside, g, 0)
+        tile_sm[k] = tile
+        seg_sm[k] = of
+        return carry
+
+    lax.fori_loop(0, RELAYED, plan_over, 0)
+    ends, begins, overs = [], [], []
     total = jnp.int32(0)
     for r in range(N_DP):
         begins.append(total)
+        overs.append(over_sm[(mine - r + N_DP) % N_DP])
         total = total + seg[(mine - r + N_DP) % N_DP]
         ends.append(total)
 
@@ -184,7 +209,10 @@
         for r in range(N_DP):
             begins_here = begins_here | (start_of[r] == k)
             inside = (k >= begins[r]) & (k < ends[r])
-            pick = pick + jnp.where(inside, r * SEG_MOST + k - begins[r], 0)
+            within = k - begins[r]
+            place = jnp.where(within < DIRECT, r * DIRECT + within,
+                              N_DP * DIRECT + overs[r] + within - DIRECT)
+            pick = pick + jnp.where(inside, place, 0)
         first = jnp.where(begins_here, k, first)
         first_sm[k] = first
         pick_sm[k] = pick
@@ -199,42 +227,60 @@
     wts[:, 3 * BLK : 4 * BLK] = jnp.where(lane < HALF, turned, 0.0).astype(jnp.bfloat16)
     wts[:, 4 * BLK :] = kv_up[:, 3 * BLK :]
     kext[:, :LEAD, :] = jnp.zeros((2, LEAD, 2 * BLK), jnp.bfloat16)
-    vext[:, :LEAD, :] = jnp.zeros((2, LEAD, 2 * BLK), jnp.bfloat16)
-
-    for d in range(1, 4):
-        got = xall.at[(y + NY - d) % NY, :, c, 0]
+    vext[:, :LEAD, :BLK] = jnp.zeros((2, LEAD, BLK), jnp.bfloat16)
+    vext[:, :, BLK:] = jnp.ones((2, LEAD + NBLK * BLK, BLK), jnp.bfloat16)
+
+    lane4 = lax.broadcasted_iota(jnp.int32, (NX * NC * HALF, BLK), 1)
+
+    def project(half, held, chips):
+        block = held[...].reshape(NX * NC * HALF, XW)
+        rot = block[:, LAT:].astype(jnp.float32)
+        kv = jnp.dot(block[:, :LAT], wts[...], preferred_element_type=jnp.float32)
+        k0 = kv[:, :BLK].astype(jnp.bfloat16)
+        r0 = jnp.where(lane4 < HALF, rot, 0.0).astype(jnp.bfloat16)
+        v0 = kv[:, BLK : 2 * BLK].astype(jnp.bfloat16)
+        k1 = kv[:, 2 * BLK : 3 * BLK].astype(jnp.bfloat16)
+        r1 = jnp.where(lane4 < HALF, kv[:, 3 * BLK : 4 * BLK], rot).astype(jnp.bfloat16)
+        v1 = kv[:, 4 * BLK :].astype(jnp.bfloat16)
+        for p in range(NX):
+            for q in range(NC):
+                chip = chips * NX + p if half == 0 else p * NX + chips
+                begin = LEAD + (chip * NC + q) * BLK + half * HALF
+                at = pl.ds(pl.multiple_of(begin, HALF), HALF)
+                of = slice((p * NC + q) * HALF, (p * NC + q + 1) * HALF)
+                kext[0, at, :BLK] = k0[of]
+                kext[0, at, BLK:] = r0[of]
+                vext[0, at, :BLK] = v0[of]
+                kext[1, at, :BLK] = k1[of]
+                kext[1, at, BLK:] = r1[of]
+                vext[1, at, :BLK] = v1[of]
+
+    def pass_on(d):
+        got = xa[d].at[:, c]
         remote(got, got, l2_send.at[0, d], l2_recv.at[0, d], seq=at_y(d)).wait_recv()
         sib.append(remote(got, got, sib_send.at[0, d], sib_recv.at[0, d], seq=sibling))
         sib[-1].start()
-        got = xall.at[:, (x + NX - d) % NX, c, 1]
+        got = xb[d].at[:, c]
         remote(got, got, l2_send.at[1, d], l2_recv.at[1, d], seq=at_x(d)).wait_recv()
         sib.append(remote(got, got, sib_send.at[1, d], sib_recv.at[1, d], seq=sibling))
         sib[-1].start()
-    for d in range(4):
-        got = xall.at[(y + NY - d) % NY, :, 1 - c, 0]
+
+    def take_in(d):
+        got = xa[d].at[:, 1 - c]
         remote(got, got, sib_send.at[0, d], sib_recv.at[0, d], seq=sibling).wait_recv()
-        got = xall.at[:, (x + NX - d) % NX, 1 - c, 1]
+        project(0, xa[d], (y + NY - d) % NY)
+        got = xb[d].at[:, 1 - c]
         remote(got, got, sib_send.at[1, d], sib_recv.at[1, d], seq=sibling).wait_recv()
-
-    lane2 = lax.broadcasted_iota(jnp.int32, (2 * BLK, BLK), 1)
-
-    def project(i, carry):
-        block = xall[i // NX, i % NX].reshape(2 * BLK, XW)
-        rot = block[:, LAT:].astype(jnp.float32)
-        kv = jnp.dot(block[:, :LAT], wts[...], preferred_element_type=jnp.float32)
-        at = pl.ds(pl.multiple_of(LEAD + i * 2 * BLK, BLK), 2 * BLK)
-        ones = jnp.ones((2 * BLK, BLK), jnp.bfloat16)
-        kext[0, at, :BLK] = kv[:, :BLK].astype(jnp.bfloat16)
-        kext[0, at, BLK:] = jnp.where(lane2 < HALF, rot, 0.0).astype(jnp.bfloat16)
-        vext[0, at, :BLK] = kv[:, BLK : 2 * BLK].astype(jnp.bfloat16)
-        vext[0, at, BLK:] = ones
-        kext[1, at, :BLK] = kv[:, 2 * BLK : 3 * BLK].astype(jnp.bfloat16)
-        kext[1, at, BLK:] = jnp.where(lane2 < HALF, kv[:, 3 * BLK : 4 * BLK], rot).astype(jnp.bfloat16)
-        vext[1, at, :BLK] = kv[:, 4 * BLK :].astype(jnp.bfloat16)
-        vext[1, at, BLK:] = ones
-        return carry
-
-    lax.fori_loop(0, NBLK // 2, project, 0)
+        project(1, xb[d], (x + NX - d) % NX)
+
+    take_in(0)
+    pass_on(1)
+    pass_on(3)
+    take_in(1)
+    pass_on(2)
+    q_start(1)
+    take_in(3)
+    take_in(2)
     q_start(2)
     q_start(3)
 
@@ -276,22 +322,75 @@
 
         lax.fori_loop(0, NBLK // GROUP, body, 0, unroll=2)
 
-    def z_copy(r, d, slot):
-        return remote(zsend.at[r, d], zrecv[r].at[slot], z_send.at[r, d], z_recv.at[r, d],
+    rest = PIECE - HALF
+
+    def z_copy(r, d, source):
+        return remote(zsend.at[r, d], zrecv[r].at[pl.ds(source * DIRECT, DIRECT)],
+                      z_send.at[r, d], z_recv.at[r, d], dp=(s + d) % N_DP)
+
+    def r_copy(r, d, source):
+        return remote(rsend.at[r, d], rrecv[r].at[source], r_send.at[r, d], r_recv.at[r, d],
                       dp=(s + d) % N_DP)
+
+    def f_places(r, relay):
+        places = [zrecv[r].at[N_DP * DIRECT + relay]]
+        if rest:
+            part = pl.ds(pl.multiple_of(relay % 2 * rest, rest), rest)
+            places.append(zrecv[r].at[N_DP * DIRECT + N_DP + relay // 2, part])
+        return places
+
+    def f_copies(r, d, relay):
+        places = f_places(r, relay)
+        pieces = [fsend.at[r, d, pl.ds(0, HALF)]]
+        if rest:
+            pieces.append(fsend.at[r, d, pl.ds(HALF, rest)])
+        return [remote(a, b, f_send.at[r, e, d], f_recv.at[r, e, d], dp=(s + d) % N_DP)
+                for e, (a, b) in enumerate(zip(pieces, places))]
+
+    def send_relays(r):
+        for d in Z_ORDER:
+            relay = (s + d) % N_DP
+            dst = rrecv[r].at[s] if d == 0 else rsend.at[r, d]
+            dst[:HALF] = att[tile_sm[relay]]
+            if rest:
+                part = pl.ds(pl.multiple_of(relay % 2 * rest, rest), rest)
+                dst[HALF:] = att[tile_sm[N_DP + relay // 2], part]
+            if d:
+                r_copy(r, d, s).start()
 
     def send_dp(r):
         for d in Z_ORDER:
             base = slot_sm[d]
-            for j in range(SEG_MOST):
+            for j in range(DIRECT):
                 tile = att[jnp.minimum(base + j, NBLK - 1)]
                 if d == 0:
-                    zrecv[r][s, j] = tile
+                    zrecv[r][s * DIRECT + j] = tile
                 else:
                     zsend[r, d, j] = tile
             if d:
                 z_copy(r, d, s).start()
 
+    def forward(r):
+        for d in range(1, N_DP):
+            r_copy(r, d, (s + N_DP - d) % N_DP).wait_recv()
+        for d in Z_ORDER:
+            source = (inv_sm[d] - seg_sm[s] + N_DP) % N_DP
+            tile = rrecv[r][source, :HALF]
+            if rest:
+                source = (inv_sm[d] - seg_sm[N_DP + s // 2] + N_DP) % N_DP
+                more = rrecv[r][source, HALF:]
+            if d:
+                fsend[r, d, :HALF] = tile
+                if rest:
+                    fsend[r, d, HALF:] = more
+                for cp in f_copies(r, d, s):
+                    cp.start()
+            else:
+                places = f_places(r, s)
+                places[0][...] = tile
+                if rest:
+                    places[1][...] = more
+
     def o_part(r, owner):
         begin = pl.multiple_of((2 * owner + r // 2) * BLK, BLK)
         return out.at[pl.ds(r % 2 * HALF, HALF), pl.ds(begin, BLK)]
@@ -305,20 +404,25 @@
     def send_seq(r):
         for d in range(1, N_DP):
             z_copy(r, d, (s + N_DP - d) % N_DP).wait_recv()
+            for cp in f_copies(r, d, (s + N_DP - d) % N_DP):
+                cp.wait_recv()
         for o in ORDER:
             peer = seq_peer(y, x, c, o)
-            pick = pick_sm[peer]
-            osend[r, o] = zrecv[r][pick // SEG_MOST, pick % SEG_MOST]
+            osend[r, o] = zrecv[r][pick_sm[peer]]
             o_copy(r, o, me, peer).start()
-        pick = pick_sm[me]
-        osend[r, 0] = zrecv[r][pick // SEG_MOST, pick % SEG_MOST]
+        osend[r, 0] = zrecv[r][pick_sm[me]]
         o_own(r).start()
 
     for r in range(ROUNDS):
         q_arrive(r)
         attend(r)
+        if r:
+            forward(r - 1)
+        send_relays(r)
         send_dp(r)
-    for r in range(ROUNDS):
+    send_seq(0)
+    forward(ROUNDS - 1)
+    for r in range(1, ROUNDS):
         send_seq(r)
 
     for cp in ph1 + ph2 + ph2b + sib:
@@ -326,7 +430,8 @@
     for r in range(ROUNDS):
         q_drain(r)
         for d in range(1, N_DP):
-            z_copy(r, d, s).wait_send()
+            for cp in [z_copy(r, d, s), r_copy(r, d, s)] + f_copies(r, d, s):
+                cp.wait_send()
         o_own(r).wait()
 
         def body(o, carry):
@@ -351,23 +456,26 @@
         in_specs=[anywhere, vmem, vmem, vmem, vmem, smem, smem, smem],
         out_specs=anywhere,
         scratch_shapes=[
-            pltpu.VMEM((NY, NX, NC, 2, HALF, XW), bf16),
+            *[pltpu.VMEM((NX, NC, HALF, XW), bf16)] * 8,
             pltpu.VMEM((2, NBLK, HALF, 2 * BLK), bf16),
             pltpu.VMEM((2, NBLK, HALF, BLK), bf16),
             pltpu.VMEM((LAT, 5 * BLK), bf16),
             pltpu.VMEM((2, LEAD + NBLK * BLK, 2 * BLK), bf16),
             pltpu.VMEM((2, LEAD + NBLK * BLK, 2 * BLK), bf16),
             pltpu.VMEM((NBLK, HALF, BLK), bf16),
-            pltpu.VMEM((ROUNDS, N_DP, SEG_MOST, HALF, BLK), bf16),
-            *[pltpu.VMEM((N_DP, SEG_MOST, HALF, BLK), bf16)] * ROUNDS,
+            pltpu.VMEM((ROUNDS, N_DP, DIRECT, HALF, BLK), bf16),
+            *[pltpu.VMEM((N_DP * DIRECT + RELAYED, HALF, BLK), bf16)] * ROUNDS,
+            pltpu.VMEM((ROUNDS, N_DP, PIECE, BLK), bf16),
+            *[pltpu.VMEM((N_DP, PIECE, BLK), bf16)] * ROUNDS,
+            pltpu.VMEM((ROUNDS, N_DP, PIECE, BLK), bf16),
             pltpu.VMEM((ROUNDS, N_SEQ, HALF, BLK), bf16),
-            pltpu.SMEM((N_DP,), jnp.int32),
-            pltpu.SMEM((NBLK,), jnp.int32),
-            pltpu.SMEM((NBLK,), jnp.int32),
-            pltpu.SMEM((N_DP,), jnp.int32),
+            *[pltpu.SMEM((n,), jnp.int32)
+              for n in (N_DP, NBLK, NBLK, N_DP, N_DP, RELAYED, RELAYED, N_DP)],
             dma((2, 4)), dma((2, 4)), dma((2, 4)), dma((2, 4)), dma((2, 4)), dma((2, 4)),
             dma((ROUNDS, N_SEQ)), dma((ROUNDS, N_SEQ)),
             dma((ROUNDS, N_DP)), dma((ROUNDS, N_DP)),
+            dma((ROUNDS, N_DP)), dma((ROUNDS, N_DP)),
+            dma((ROUNDS, 2, N_DP)), dma((ROUNDS, 2, N_DP)),
             dma((ROUNDS, N_SEQ)), dma((ROUNDS, N_SEQ)),
             dma((2 * ROUNDS,)),
         ],

time: 173 us -> 153 us (0.88)
  Pallas kernels: 168 us -> 148 us
    pallas_call x1, Pallas kernels: 168 us -> 148 us  [on_device(): pl.pallas_call(kernel, out_shape=jax.ShapeDtypeStruct((BLK, N_SEQ * 2 * H...]
where the time goes in v3:
time: 153 us
  Pallas kernels  148 us (97%)
  local copies, waits for them, and re-layouts  3.92 us (3%)
    pallas_call x1, Pallas kernels, on_device(): pl.pallas_call(kernel, out_shape=jax.ShapeDtypeStruct((BLK, N_SEQ * 2 * H...  148 us
    unnamed x2, local copies, waits for them, and re-layouts  3.92 us

profile of v3, /device:TPU:1, one launch (start us, length us, event | category | flops | bytes accessed | tf_op | source)
XLA Modules:
  0.0 153.0 jit_solution(9478482711398384466)
XLA Ops:
  0.0 0.8 copy.9
  0.8 0.7 pad_maximum_fusion.rope2
  1.5 148.3 %shard_map.82 = bf16[128,8192]{1,0:T(8,128)(2,1)} custom-call(bf16[128,12288]{1,0:T(8,128)(2,1)} %queries.1, bf16[128,512]{1,0:T(8,128)(2,1)} %latent.1, bf16[128,128]{1,0:T(8,128)(2,1)} %pad_maximum_fusion.rope2, f32[1,512]{1,0:T(1,128)} %bitcast.1, bf16[512,512]{1,0:T(8,128)(2,1)} %kv_up.1, s32[8]{0:T(128)} %seg.1, s32[8]{0:T(128)} %bucket_of.1, ...), custom_call_target="tpu_custom_call" | custom-call | tf_op jit(solution)/shard_map/pallas_call | solution.py:453
  149.9 3.1 %copy.12 = bf16[128,8192]{1,0:T(8,128)(2,1)} copy(bf16[128,8192]{1,0:T(8,128)(2,1)} %shard_map.82) | data formatting | bytes 4194304

commit v4 on v3

--- a/solution.py
+++ b/solution.py
@@ -27,9 +27,9 @@
 ORDER = (20, 21, 12, 24, 13, 25, 18, 6, 19, 7, 22, 2, 23, 3, 28, 8, 29, 9, 4, 16, 5, 17, 10, 30, 11, 31, 14, 26, 15, 27, 1)
 Z_ORDER = (4, 3, 5, 2, 6, 1, 7, 0)
 EARLY = 10
+NEAR = (1, 3, 2)
 DIRECT = 4
-RELAYED = 12
-PIECE = HALF + (RELAYED - N_DP) * HALF // N_DP
+RELAYS = (8, 12)
 EPS = 1e-06
 NEG = -1e30
 EXP_SCALE = (HD_NOPE + HD_ROPE) ** -0.5 * math.log2(math.e)
@@ -46,7 +46,8 @@
 
 
 def kernel(
-    queries, latent, rope2, gain, kv_up, seg, bucket_of, breaks,
+    relayed,
+    queries, latent, rope_t, gain, kv_up, seg, bucket_of, breaks,
     out,
     xa0, xa1, xa2, xa3, xb0, xb1, xb2, xb3, qa, qb, wts, kext, vext, att, zsend, zrecv0, zrecv1, zrecv2, zrecv3, rsend, rrecv0, rrecv1, rrecv2, rrecv3, fsend, osend,
     starts_sm, first_sm, pick_sm, slot_sm, over_sm, tile_sm, seg_sm, inv_sm,
@@ -83,7 +84,9 @@
     normed = (
         lat * lax.rsqrt(jnp.mean(lat * lat, axis=1, keepdims=True) + EPS) * gain[...]
     ).astype(jnp.bfloat16)
-    rows = jnp.concatenate([normed, rope2[...]], axis=1)
+    rope = rope_t[...].astype(jnp.float32)
+    rope2 = jnp.transpose(jnp.concatenate([rope, rope], axis=0)).astype(jnp.bfloat16)
+    rows = jnp.concatenate([normed, rope2], axis=1)
     xa0[x, c] = rows[:HALF]
     xb0[y, c] = rows[HALF:]
 
@@ -96,13 +99,29 @@
         return ((y + d) % NY) * (NX * NC) + x * NC + c
 
     sibling = y * (NX * NC) + x * NC + (1 - c)
-    ph1 = []
-    for d in range(1, 4):
-        own_a, own_b = xa0.at[x, c], xb0.at[y, c]
-        ph1.append(remote(own_a, own_a, l1_send.at[0, d], l1_recv.at[0, d], seq=at_x(d)))
-        ph1.append(remote(own_b, own_b, l1_send.at[1, d], l1_recv.at[1, d], seq=at_y(d)))
-    for cp in ph1:
-        cp.start()
+    def ph1_copy(half, d, place):
+        ref = xa0.at[place, c] if half == 0 else xb0.at[place, c]
+        return remote(ref, ref, l1_send.at[half, d], l1_recv.at[half, d], seq=at_x(d) if half == 0 else at_y(d))
+
+    def ph2_copy(half, d, p):
+        if half == 0:
+            place = (x + NX - p) % NX
+            src, dst, peer = xa0.at[place, c], xa[d].at[place, c], at_y(d)
+        else:
+            place = (y + NY - p) % NY
+            src, dst, peer = xb0.at[place, c], xb[d].at[place, c], at_x(d)
+        return remote(src, dst, l2_send.at[half, d, p], l2_recv.at[half, d, p], seq=peer)
+
+    def sib_copy(half, d):
+        ref = (xa if half == 0 else xb)[d].at[:, c]
+        return remote(ref, ref, sib_send.at[half, d], sib_recv.at[half, d], seq=sibling)
+
+    for d in NEAR:
+        ph1_copy(0, d, x).start()
+        ph1_copy(1, d, y).start()
+    for d in NEAR:
+        ph2_copy(0, d, 0).start()
+        ph2_copy(1, d, 0).start()
 
     def q_copy(r, o, peer, slot):
         h, half = r // 2, r % 2
@@ -140,26 +159,15 @@
     for r in range(ROUNDS):
         q_own(r).start()
 
-    for d in range(1, 4):
-        there = xa0.at[(x + NX - d) % NX, c]
-        remote(there, there, l1_send.at[0, d], l1_recv.at[0, d], seq=at_x(d)).wait_recv()
-    row_a = xa0.at[:, c]
-    ph2 = [remote(row_a, xa[d].at[:, c], l2_send.at[0, d], l2_recv.at[0, d], seq=at_y(d)) for d in range(1, 4)]
-    for cp in ph2:
-        cp.start()
-    for d in range(1, 4):
-        there = xb0.at[(y + NY - d) % NY, c]
-        remote(there, there, l1_send.at[1, d], l1_recv.at[1, d], seq=at_y(d)).wait_recv()
-    col_b = xb0.at[:, c]
-    ph2b = [remote(col_b, xb[d].at[:, c], l2_send.at[1, d], l2_recv.at[1, d], seq=at_x(d)) for d in range(1, 4)]
-    for cp in ph2b:
-        cp.start()
-    sib = [
-        remote(row_a, row_a, sib_send.at[0, 0], sib_recv.at[0, 0], seq=sibling),
-        remote(col_b, col_b, sib_send.at[1, 0], sib_recv.at[1, 0], seq=sibling),
-    ]
-    for cp in sib:
-        cp.start()
+    for p in NEAR:
+        ph1_copy(0, p, (x + NX - p) % NX).wait_recv()
+        for d in NEAR:
+            ph2_copy(0, d, p).start()
+        ph1_copy(1, p, (y + NY - p) % NY).wait_recv()
+        for d in NEAR:
+            ph2_copy(1, d, p).start()
+    for half in range(2):
+        sib_copy(half, 0).start()
 
     q_start(0, ORDER[EARLY:])
 
@@ -194,7 +202,7 @@
         seg_sm[k] = of
         return carry
 
-    lax.fori_loop(0, RELAYED, plan_over, 0)
+    lax.fori_loop(0, relayed, plan_over, 0)
     ends, begins, overs = [], [], []
     total = jnp.int32(0)
     for r in range(N_DP):
@@ -256,22 +264,16 @@
                 vext[1, at, :BLK] = v1[of]
 
     def pass_on(d):
-        got = xa[d].at[:, c]
-        remote(got, got, l2_send.at[0, d], l2_recv.at[0, d], seq=at_y(d)).wait_recv()
-        sib.append(remote(got, got, sib_send.at[0, d], sib_recv.at[0, d], seq=sibling))
-        sib[-1].start()
-        got = xb[d].at[:, c]
-        remote(got, got, l2_send.at[1, d], l2_recv.at[1, d], seq=at_x(d)).wait_recv()
-        sib.append(remote(got, got, sib_send.at[1, d], sib_recv.at[1, d], seq=sibling))
-        sib[-1].start()
+        for half in range(2):
+            for p in range(4):
+                ph2_copy(half, d, p).wait_recv()
+            sib_copy(half, d).start()
 
     def take_in(d):
-        got = xa[d].at[:, 1 - c]
-        remote(got, got, sib_send.at[0, d], sib_recv.at[0, d], seq=sibling).wait_recv()
-        project(0, xa[d], (y + NY - d) % NY)
-        got = xb[d].at[:, 1 - c]
-        remote(got, got, sib_send.at[1, d], sib_recv.at[1, d], seq=sibling).wait_recv()
-        project(1, xb[d], (x + NX - d) % NX)
+        for half in range(2):
+            got = (xa if half == 0 else xb)[d].at[:, 1 - c]
+            remote(got, got, sib_send.at[half, d], sib_recv.at[half, d], seq=sibling).wait_recv()
+            project(half, (xa if half == 0 else xb)[d], (((y + NY) if half == 0 else (x + NX)) - d) % 4)
 
     take_in(0)
     pass_on(1)
@@ -317,12 +319,12 @@
             o = jnp.dot(jnp.concatenate(parts, axis=0), vext[h, at, :],
                         preferred_element_type=jnp.float32)
             o = (o[:, :BLK] / o[:, BLK:]).astype(jnp.bfloat16)
-            att[of] = o.reshape(GROUP, HALF, BLK)
+            att[r, of] = o.reshape(GROUP, HALF, BLK)
             return carry
 
         lax.fori_loop(0, NBLK // GROUP, body, 0, unroll=2)
 
-    rest = PIECE - HALF
+    rest = (relayed - N_DP) * HALF // N_DP
 
     def z_copy(r, d, source):
         return remote(zsend.at[r, d], zrecv[r].at[pl.ds(source * DIRECT, DIRECT)],
@@ -351,10 +353,10 @@
         for d in Z_ORDER:
             relay = (s + d) % N_DP
             dst = rrecv[r].at[s] if d == 0 else rsend.at[r, d]
-            dst[:HALF] = att[tile_sm[relay]]
+            dst[:HALF] = att[r, tile_sm[relay]]
             if rest:
                 part = pl.ds(pl.multiple_of(relay % 2 * rest, rest), rest)
-                dst[HALF:] = att[tile_sm[N_DP + relay // 2], part]
+                dst[HALF:] = att[r, tile_sm[N_DP + relay // 2], part]
             if d:
                 r_copy(r, d, s).start()
 
@@ -362,7 +364,7 @@
         for d in Z_ORDER:
             base = slot_sm[d]
             for j in range(DIRECT):
-                tile = att[jnp.minimum(base + j, NBLK - 1)]
+                tile = att[r, jnp.minimum(base + j, NBLK - 1)]
                 if d == 0:
                     zrecv[r][s * DIRECT + j] = tile
                 else:
@@ -416,17 +418,24 @@
     for r in range(ROUNDS):
         q_arrive(r)
         attend(r)
+        send_relays(r)
+        if r != 1:
+            send_dp(max(r - 1, 0))
         if r:
             forward(r - 1)
-        send_relays(r)
-        send_dp(r)
+    send_dp(ROUNDS - 1)
     send_seq(0)
     forward(ROUNDS - 1)
     for r in range(1, ROUNDS):
         send_seq(r)
 
-    for cp in ph1 + ph2 + ph2b + sib:
-        cp.wait_send()
+    for half in range(2):
+        for d in range(4):
+            sib_copy(half, d).wait_send()
+        for d in NEAR:
+            ph1_copy(half, d, y if half else x).wait_send()
+            for p in range(4):
+                ph2_copy(half, d, p).wait_send()
     for r in range(ROUNDS):
         q_drain(r)
         for d in range(1, N_DP):
@@ -443,15 +452,15 @@
         lax.fori_loop(1, N_SEQ, body, 0)
 
 
-def on_device(queries, kv_latent, key_rope, kv_gain, kv_up, segment_blocks, bucket_of, doc_breaks):
+def call(relayed, index):
     bf16 = jnp.bfloat16
-    rope2 = jnp.concatenate([key_rope, key_rope], axis=1)
+    piece = HALF + (relayed - N_DP) * HALF // N_DP
     vmem = pl.BlockSpec(memory_space=pltpu.VMEM)
     smem = pl.BlockSpec(memory_space=pltpu.SMEM)
     anywhere = pl.BlockSpec(memory_space=pl.ANY)
     dma = pltpu.SemaphoreType.DMA
     return pl.pallas_call(
-        kernel,
+        functools.partial(kernel, relayed),
         out_shape=jax.ShapeDtypeStruct((BLK, N_SEQ * 2 * HD_V), bf16),
         in_specs=[anywhere, vmem, vmem, vmem, vmem, smem, smem, smem],
         out_specs=anywhere,
@@ -462,16 +471,16 @@
             pltpu.VMEM((LAT, 5 * BLK), bf16),
             pltpu.VMEM((2, LEAD + NBLK * BLK, 2 * BLK), bf16),
             pltpu.VMEM((2, LEAD + NBLK * BLK, 2 * BLK), bf16),
-            pltpu.VMEM((NBLK, HALF, BLK), bf16),
+            pltpu.VMEM((ROUNDS, NBLK, HALF, BLK), bf16),
             pltpu.VMEM((ROUNDS, N_DP, DIRECT, HALF, BLK), bf16),
-            *[pltpu.VMEM((N_DP * DIRECT + RELAYED, HALF, BLK), bf16)] * ROUNDS,
-            pltpu.VMEM((ROUNDS, N_DP, PIECE, BLK), bf16),
-            *[pltpu.VMEM((N_DP, PIECE, BLK), bf16)] * ROUNDS,
-            pltpu.VMEM((ROUNDS, N_DP, PIECE, BLK), bf16),
+            *[pltpu.VMEM((N_DP * DIRECT + relayed, HALF, BLK), bf16)] * ROUNDS,
+            pltpu.VMEM((ROUNDS, N_DP, piece, BLK), bf16),
+            *[pltpu.VMEM((N_DP, piece, BLK), bf16)] * ROUNDS,
+            pltpu.VMEM((ROUNDS, N_DP, piece, BLK), bf16),
             pltpu.VMEM((ROUNDS, N_SEQ, HALF, BLK), bf16),
             *[pltpu.SMEM((n,), jnp.int32)
-              for n in (N_DP, NBLK, NBLK, N_DP, N_DP, RELAYED, RELAYED, N_DP)],
-            dma((2, 4)), dma((2, 4)), dma((2, 4)), dma((2, 4)), dma((2, 4)), dma((2, 4)),
+              for n in (N_DP, NBLK, NBLK, N_DP, N_DP, relayed, relayed, N_DP)],
+            dma((2, 4)), dma((2, 4)), dma((2, 4, 4)), dma((2, 4, 4)), dma((2, 4)), dma((2, 4)),
             dma((ROUNDS, N_SEQ)), dma((ROUNDS, N_SEQ)),
             dma((ROUNDS, N_DP)), dma((ROUNDS, N_DP)),
             dma((ROUNDS, N_DP)), dma((ROUNDS, N_DP)),
@@ -480,9 +489,17 @@
             dma((2 * ROUNDS,)),
         ],
         compiler_params=pltpu.CompilerParams(
-            collective_id=0, has_side_effects=True, vmem_limit_bytes=56 * 2**20
+            collective_id=index, has_side_effects=True, vmem_limit_bytes=56 * 2**20
         ),
-    )(queries, kv_latent, rope2, kv_gain.reshape(1, LAT), kv_up, segment_blocks, bucket_of, doc_breaks)
+    )
+
+
+def on_device(queries, kv_latent, key_rope, kv_gain, kv_up, segment_blocks, bucket_of, doc_breaks):
+    over = jnp.sum(jnp.maximum(segment_blocks - DIRECT, 0))
+    return lax.cond(
+        over <= RELAYS[0], call(RELAYS[0], 0), call(RELAYS[1], 1),
+        queries, kv_latent, key_rope.T, kv_gain.reshape(1, LAT), kv_up, segment_blocks, bucket_of, doc_breaks,
+    )
 
 
 def solution(mesh):

time: 153 us -> 142 us (0.928)
  Pallas kernels: 148 us -> 138 us
  local copies, waits for them, and re-layouts: 3.92 us -> 1.32 us
    pallas_call x1, Pallas kernels: 148 us -> 138 us  [on_device(): lax.cond(over <= RELAYS[0], call(RELAYS[0], 0), call(RELAYS[1], 1), queri...]
    unnamed x2 -> x1, local copies, waits for them, and re-layouts: 3.92 us -> 1.32 us
where the time goes in v4:
time: 142 us
  Pallas kernels  138 us (97%)
    pallas_call x1, Pallas kernels, on_device(): lax.cond(over <= RELAYS[0], call(RELAYS[0], 0), call(RELAYS[1], 1), queri...  138 us

profile of v4, /device:TPU:1, one launch (start us, length us, event | category | flops | bytes accessed | tf_op | source)
XLA Modules:
  0.0 141.7 jit_solution(5266117199295085834)
XLA Ops:
  0.0 1.3 maximum_reduce_fusion
  1.9 138.5 %conditional.1 = (bf16[128,8192]{1,0:T(8,128)(2,1)S(1)}) conditional(s32[]{:T(128)} %convert_element_type.3, (bf16[128,12288]{1,0:T(8,128)(2,1)}, bf16[128,512]{1,0:T(8,128)(2,1)}, bf16[64,128]{1,0:T(8,128)(2,1)}, f32[512]{0:T(512)}, bf16[512,512]{1,0:T(8,128)(2,1)}, /*index=5*/s32[8]{0:T(128)}, s32[8]{0:T(128)}, s32[8,32]{1,0:T(8,128)}) %tuple.16, ...), branch_computations={%region_1.0_spmd, %region_2.0_spmd} | conditional | bytes 8 | solution.py:499
  2.2 137.9 %branch_1_fun.1 = bf16[128,8192]{1,0:T(8,128)(2,1)S(1)} custom-call(bf16[128,12288]{1,0:T(8,128)(2,1)} %get-tuple-element.70.queries, bf16[128,512]{1,0:T(8,128)(2,1)} %get-tuple-element.72.latent, bf16[64,128]{1,0:T(8,128)(2,1)} %get-tuple-element.50.rope_t, f32[1,512]{1,0:T(1,128)} %bitcast.6, bf16[512,512]{1,0:T(8,128)(2,1)} %get-tuple-element.76.kv_up, ...), custom_call_target="tpu_custom_call" | custom-call | tf_op jit(solution)/shard_map/cond/branch_1_fun/pallas_call | solution.py:499
  140.4 1.3 copy.26

commit v5 on v4

--- a/solution.py
+++ b/solution.py
@@ -128,25 +128,22 @@
         width = BLK if h else 2 * BLK
         begin = pl.multiple_of(peer * (3 * BLK) + h * 2 * BLK, BLK)
         return remote(queries.at[pl.ds(half * HALF, HALF), pl.ds(begin, width)],
-                      (qb if h else qa).at[half, slot], q_send.at[r, o], q_recv.at[r, o], seq=peer)
+                      (qb if h else qa).at[half, slot], q_send.at[r], q_recv.at[r], seq=peer)
 
     def q_start(r, order=ORDER):
         for o in order:
             q_copy(r, o, seq_peer(y, x, c, o), me).start()
 
+    def all_of(ref, sem):
+        part = ref.at[pl.ds(0, N_SEQ - 1)]
+        return pltpu.make_async_copy(part, part, sem)
+
     def q_arrive(r):
         q_own(r).wait()
-
-        def body(o, carry):
-            q_copy(r, o, seq_peer(y, x, c, o), seq_source(y, x, c, o)).wait_recv()
-            return carry
-        lax.fori_loop(1, N_SEQ, body, 0)
+        all_of((qb if r // 2 else qa).at[r % 2], q_recv.at[r]).wait()
 
     def q_drain(r):
-        def body(o, carry):
-            q_copy(r, o, seq_peer(y, x, c, o), me).wait_send()
-            return carry
-        lax.fori_loop(1, N_SEQ, body, 0)
+        all_of((qb if r // 2 else qa).at[r % 2], q_send.at[r]).wait()
 
     def q_own(r):
         h, half = r // 2, r % 2
@@ -279,12 +276,10 @@
     pass_on(1)
     pass_on(3)
     take_in(1)
+    q_start(1)
     pass_on(2)
-    q_start(1)
     take_in(3)
     take_in(2)
-    q_start(2)
-    q_start(3)
 
     row_id = lax.broadcasted_iota(jnp.int32, (HALF, BLK), 0)
     col_id = lax.broadcasted_iota(jnp.int32, (HALF, BLK), 1)
@@ -398,7 +393,7 @@
         return out.at[pl.ds(r % 2 * HALF, HALF), pl.ds(begin, BLK)]
 
     def o_copy(r, o, owner, peer):
-        return remote(osend.at[r, o], o_part(r, owner), o_send.at[r, o], o_recv.at[r, o], seq=peer)
+        return remote(osend.at[r, o], o_part(r, owner), o_send.at[r], o_recv.at[r], seq=peer)
 
     def o_own(r):
         return pltpu.make_async_copy(osend.at[r, 0], o_part(r, me), own_sem.at[ROUNDS + r])
@@ -415,41 +410,51 @@
         osend[r, 0] = zrecv[r][pick_sm[me]]
         o_own(r).start()
 
+    def gather_drain():
+        for half in range(2):
+            for d in range(4):
+                sib_copy(half, d).wait_send()
+            for d in NEAR:
+                ph1_copy(half, d, y if half else x).wait_send()
+                for p in range(4):
+                    ph2_copy(half, d, p).wait_send()
+
+    def dp_drain(r):
+        for d in range(1, N_DP):
+            for cp in [z_copy(r, d, s), r_copy(r, d, s)] + f_copies(r, d, s):
+                cp.wait_send()
+
+    def o_drain(r):
+        o_own(r).wait()
+        all_of(osend.at[r], o_send.at[r]).wait()
+        all_of(osend.at[r], o_recv.at[r]).wait()
+
     for r in range(ROUNDS):
         q_arrive(r)
         attend(r)
-        send_relays(r)
-        if r != 1:
-            send_dp(max(r - 1, 0))
         if r:
             forward(r - 1)
-    send_dp(ROUNDS - 1)
+        send_relays(r)
+        send_dp(r)
+        if r == 0:
+            q_start(2)
+            q_start(3)
+    gather_drain()
     send_seq(0)
     forward(ROUNDS - 1)
-    for r in range(1, ROUNDS):
-        send_seq(r)
-
-    for half in range(2):
-        for d in range(4):
-            sib_copy(half, d).wait_send()
-        for d in NEAR:
-            ph1_copy(half, d, y if half else x).wait_send()
-            for p in range(4):
-                ph2_copy(half, d, p).wait_send()
     for r in range(ROUNDS):
         q_drain(r)
-        for d in range(1, N_DP):
-            for cp in [z_copy(r, d, s), r_copy(r, d, s)] + f_copies(r, d, s):
-                cp.wait_send()
-        o_own(r).wait()
-
-        def body(o, carry):
-            cp = o_copy(r, o, seq_source(y, x, c, o), seq_peer(y, x, c, o))
-            cp.wait_send()
-            cp.wait_recv()
-            return carry
-
-        lax.fori_loop(1, N_SEQ, body, 0)
+    send_seq(1)
+    o_drain(0)
+    send_seq(2)
+    dp_drain(0)
+    dp_drain(1)
+    o_drain(1)
+    send_seq(3)
+    dp_drain(2)
+    dp_drain(3)
+    o_drain(2)
+    o_drain(3)
 
 
 def call(relayed, index):
@@ -481,11 +486,11 @@
             *[pltpu.SMEM((n,), jnp.int32)
               for n in (N_DP, NBLK, NBLK, N_DP, N_DP, relayed, relayed, N_DP)],
             dma((2, 4)), dma((2, 4)), dma((2, 4, 4)), dma((2, 4, 4)), dma((2, 4)), dma((2, 4)),
-            dma((ROUNDS, N_SEQ)), dma((ROUNDS, N_SEQ)),
+            dma((ROUNDS,)), dma((ROUNDS,)),
             dma((ROUNDS, N_DP)), dma((ROUNDS, N_DP)),
             dma((ROUNDS, N_DP)), dma((ROUNDS, N_DP)),
             dma((ROUNDS, 2, N_DP)), dma((ROUNDS, 2, N_DP)),
-            dma((ROUNDS, N_SEQ)), dma((ROUNDS, N_SEQ)),
+            dma((ROUNDS,)), dma((ROUNDS,)),
             dma((2 * ROUNDS,)),
         ],
         compiler_params=pltpu.CompilerParams(

time: 142 us -> 137 us (0.965)
  Pallas kernels: 138 us -> 133 us
    pallas_call x1, Pallas kernels: 138 us -> 133 us  [on_device(): lax.cond(over <= RELAYS[0], call(RELAYS[0], 0), call(RELAYS[1], 1), queri...]
where the time goes in v5:
time: 137 us
  Pallas kernels  133 us (97%)
    pallas_call x1, Pallas kernels, on_device(): lax.cond(over <= RELAYS[0], call(RELAYS[0], 0), call(RELAYS[1], 1), queri...  133 us

profile of v5, /device:TPU:1, one launch (start us, length us, event | category | flops | bytes accessed | tf_op | source)
XLA Modules:
  0.0 137.0 jit_solution(2629167583160558078)
XLA Ops:
  0.0 1.3 maximum_reduce_fusion
  1.9 133.7 %conditional.1 = (bf16[128,8192]{1,0:T(8,128)(2,1)S(1)}) conditional(s32[]{:T(128)} %convert_element_type.3, (bf16[128,12288]{1,0:T(8,128)(2,1)}, bf16[128,512]{1,0:T(8,128)(2,1)}, bf16[64,128]{1,0:T(8,128)(2,1)}, f32[512]{0:T(512)}, bf16[512,512]{1,0:T(8,128)(2,1)}, /*index=5*/s32[8]{0:T(128)}, s32[8]{0:T(128)}, s32[8,32]{1,0:T(8,128)}) %tuple.16, ...), branch_computations={%region_1.0_spmd, %region_2.0_spmd} | conditional | bytes 8 | solution.py:504
  2.2 133.4 %branch_1_fun.1 = bf16[128,8192]{1,0:T(8,128)(2,1)S(1)} custom-call(bf16[128,12288]{1,0:T(8,128)(2,1)} %get-tuple-element.70.queries, bf16[128,512]{1,0:T(8,128)(2,1)} %get-tuple-element.72.latent, bf16[64,128]{1,0:T(8,128)(2,1)} %get-tuple-element.50.rope_t, f32[1,512]{1,0:T(1,128)} %bitcast.6, bf16[512,512]{1,0:T(8,128)(2,1)} %get-tuple-element.76.kv_up, ...), custom_call_target="tpu_custom_call" | custom-call | tf_op jit(solution)/shard_map/cond/branch_1_fun/pallas_call | solution.py:504
  135.6 1.3 copy.26

commit v6 on v5

--- a/solution.py
+++ b/solution.py
@@ -134,8 +134,8 @@
         for o in order:
             q_copy(r, o, seq_peer(y, x, c, o), me).start()
 
-    def all_of(ref, sem):
-        part = ref.at[pl.ds(0, N_SEQ - 1)]
+    def all_of(ref, sem, count=N_SEQ - 1):
+        part = ref.at[pl.ds(0, count)]
         return pltpu.make_async_copy(part, part, sem)
 
     def q_arrive(r):
@@ -323,10 +323,10 @@
 
     def z_copy(r, d, source):
         return remote(zsend.at[r, d], zrecv[r].at[pl.ds(source * DIRECT, DIRECT)],
-                      z_send.at[r, d], z_recv.at[r, d], dp=(s + d) % N_DP)
+                      z_send.at[r], z_recv.at[r], dp=(s + d) % N_DP)
 
     def r_copy(r, d, source):
-        return remote(rsend.at[r, d], rrecv[r].at[source], r_send.at[r, d], r_recv.at[r, d],
+        return remote(rsend.at[r, d], rrecv[r].at[source], r_send.at[r], r_recv.at[r],
                       dp=(s + d) % N_DP)
 
     def f_places(r, relay):
@@ -341,8 +341,8 @@
         pieces = [fsend.at[r, d, pl.ds(0, HALF)]]
         if rest:
             pieces.append(fsend.at[r, d, pl.ds(HALF, rest)])
-        return [remote(a, b, f_send.at[r, e, d], f_recv.at[r, e, d], dp=(s + d) % N_DP)
-                for e, (a, b) in enumerate(zip(pieces, places))]
+        return [remote(a, b, f_send.at[r], f_recv.at[r], dp=(s + d) % N_DP)
+                for a, b in zip(pieces, places)]
 
     def send_relays(r):
         for d in Z_ORDER:
@@ -368,8 +368,7 @@
                 z_copy(r, d, s).start()
 
     def forward(r):
-        for d in range(1, N_DP):
-            r_copy(r, d, (s + N_DP - d) % N_DP).wait_recv()
+        all_of(rsend.at[r], r_recv.at[r], N_DP - 1).wait()
         for d in Z_ORDER:
             source = (inv_sm[d] - seg_sm[s] + N_DP) % N_DP
             tile = rrecv[r][source, :HALF]
@@ -399,10 +398,8 @@
         return pltpu.make_async_copy(osend.at[r, 0], o_part(r, me), own_sem.at[ROUNDS + r])
 
     def send_seq(r):
-        for d in range(1, N_DP):
-            z_copy(r, d, (s + N_DP - d) % N_DP).wait_recv()
-            for cp in f_copies(r, d, (s + N_DP - d) % N_DP):
-                cp.wait_recv()
+        all_of(zsend.at[r], z_recv.at[r], N_DP - 1).wait()
+        all_of(fsend.at[r], f_recv.at[r], N_DP - 1).wait()
         for o in ORDER:
             peer = seq_peer(y, x, c, o)
             osend[r, o] = zrecv[r][pick_sm[peer]]
@@ -420,9 +417,8 @@
                     ph2_copy(half, d, p).wait_send()
 
     def dp_drain(r):
-        for d in range(1, N_DP):
-            for cp in [z_copy(r, d, s), r_copy(r, d, s)] + f_copies(r, d, s):
-                cp.wait_send()
+        for ref, sem in ((zsend, z_send), (rsend, r_send), (fsend, f_send)):
+            all_of(ref.at[r], sem.at[r], N_DP - 1).wait()
 
     def o_drain(r):
         o_own(r).wait()
@@ -487,9 +483,9 @@
               for n in (N_DP, NBLK, NBLK, N_DP, N_DP, relayed, relayed, N_DP)],
             dma((2, 4)), dma((2, 4)), dma((2, 4, 4)), dma((2, 4, 4)), dma((2, 4)), dma((2, 4)),
             dma((ROUNDS,)), dma((ROUNDS,)),
-            dma((ROUNDS, N_DP)), dma((ROUNDS, N_DP)),
-            dma((ROUNDS, N_DP)), dma((ROUNDS, N_DP)),
-            dma((ROUNDS, 2, N_DP)), dma((ROUNDS, 2, N_DP)),
+            dma((ROUNDS,)), dma((ROUNDS,)),
+            dma((ROUNDS,)), dma((ROUNDS,)),
+            dma((ROUNDS,)), dma((ROUNDS,)),
             dma((ROUNDS,)), dma((ROUNDS,)),
             dma((2 * ROUNDS,)),
         ],

time: 137 us -> 135 us (0.985)
  Pallas kernels: 133 us -> 131 us
    pallas_call x1, Pallas kernels: 133 us -> 131 us  [on_device(): lax.cond(over <= RELAYS[0], call(RELAYS[0], 0), call(RELAYS[1], 1), queri...]
where the time goes in v6:
time: 135 us
  Pallas kernels  131 us (97%)
    pallas_call x1, Pallas kernels, on_device(): lax.cond(over <= RELAYS[0], call(RELAYS[0], 0), call(RELAYS[1], 1), queri...  131 us

profile of v6, /device:TPU:1, one launch (start us, length us, event | category | flops | bytes accessed | tf_op | source)
XLA Modules:
  0.0 134.8 jit_solution(12845804063709983554)
XLA Ops:
  0.0 1.3 maximum_reduce_fusion
  1.9 131.5 %conditional.1 = (bf16[128,8192]{1,0:T(8,128)(2,1)S(1)}) conditional(s32[]{:T(128)} %convert_element_type.3, (bf16[128,12288]{1,0:T(8,128)(2,1)}, bf16[128,512]{1,0:T(8,128)(2,1)}, bf16[64,128]{1,0:T(8,128)(2,1)}, f32[512]{0:T(512)}, bf16[512,512]{1,0:T(8,128)(2,1)}, /*index=5*/s32[8]{0:T(128)}, s32[8]{0:T(128)}, s32[8,32]{1,0:T(8,128)}) %tuple.16, ...), branch_computations={%region_1.0_spmd, %region_2.0_spmd} | conditional | bytes 8 | solution.py:500
  2.1 131.3 %branch_1_fun.1 = bf16[128,8192]{1,0:T(8,128)(2,1)S(1)} custom-call(bf16[128,12288]{1,0:T(8,128)(2,1)} %get-tuple-element.70.queries, bf16[128,512]{1,0:T(8,128)(2,1)} %get-tuple-element.72.latent, bf16[64,128]{1,0:T(8,128)(2,1)} %get-tuple-element.50.rope_t, f32[1,512]{1,0:T(1,128)} %bitcast.6, bf16[512,512]{1,0:T(8,128)(2,1)} %get-tuple-element.76.kv_up, ...), custom_call_target="tpu_custom_call" | custom-call | tf_op jit(solution)/shard_map/cond/branch_1_fun/pallas_call | solution.py:500
  133.5 1.3 copy.26
